TPU v7x, 128 devices: a whole 4x4x4 slice. The times are simulated.
128 devices in a mesh: tensor: 16 (over x_lo, y, core), replica: 8 (over z, x_hi).
Axes of the slice: x: 4 (x_hi: 2, x_lo: 2; x = x_hi * 2 + x_lo), y: 4, z: 4, core: 2. Of those that a mesh axis runs over, the one named last changes fastest.
Arguments:
- tokens: bfloat16 [5120, 4096], P(('replica', 'tensor')), may hold values from -6 to 6
- cotangent: bfloat16 [5120, 14336], P('replica', 'tensor'), may hold values from -6 to 6
- weights: bfloat16 [4096, 2, 14336], P(None, None, 'tensor'), may hold values from -0.09375 to 0.09375
- scores: float32 [4096, 2, 14336], P('replica', None, 'tensor'), may hold values from -6 to 6
- tile_mask: int32 [32, 2, 112], P(None, None, 'tensor'), may hold values 0 or 1
Outputs:
- token_grad: bfloat16 [5120, 4096], P(('replica', 'tensor'))
- weight_grad: bfloat16 [4096, 2, 14336], P('replica', None, 'tensor')
- new_scores: float32 [4096, 2, 14336], P('replica', None, 'tensor')
All inputs are finite; a program needn't handle non-finite values. No bound on the sum of `tile_mask` on one device may be relied on, other than what follows from the above.
Results may differ from a plain program's by a relative error of at most 0.023.
Values may be sent and summed in bfloat16 or wider, within the bound.
No kernel may reach another device: no remote copies, remote signals or barrier semaphores. Data moves between devices by JAX's collectives and lax.ppermute only.
A program may use at most 256 MiB of HBM per device.

v0:
```python
import math

import jax
import jax.numpy as jnp
from jax import lax
from jax.sharding import PartitionSpec as P

TILE = 128


def shards(tokens, cotangent, weights, scores, tile_mask):
    width, pair, units = weights.shape
    tile_rows, unused_pair, tile_cols = tile_mask.shape
    grown = jnp.broadcast_to(
        tile_mask[:, None, :, :, None], (tile_rows, TILE, pair, tile_cols, TILE)
    )
    keep = grown.reshape(width, pair, units)
    masked = weights * keep.astype(jnp.bfloat16)
    flat = masked.reshape(width, pair * units)
    whole = lax.all_gather(tokens, "tensor", axis=0, tiled=True)
    projected = jnp.dot(whole, flat, preferred_element_type=jnp.float32)
    gate = projected[:, :units]
    up = projected[:, units:]
    sigmoid_gate = jax.nn.sigmoid(gate)
    upstream = cotangent.astype(jnp.float32)
    gate_grad = (upstream * up * sigmoid_gate * (1.0 + gate * (1.0 - sigmoid_gate))).astype(
        jnp.bfloat16
    )
    up_grad = (upstream * gate * sigmoid_gate).astype(jnp.bfloat16)
    both_grads = jnp.concatenate([gate_grad, up_grad], axis=1)
    replicas = lax.axis_size("replica")
    total_tokens = tokens.shape[0] * lax.axis_size("tensor") * replicas
    row_count = width // replicas
    row_start = lax.axis_index("replica") * row_count
    token_grad = lax.psum_scatter(
        lax.dot_general(
            both_grads, flat, (((1,), (1,)), ((), ())), preferred_element_type=jnp.float32
        ).astype(jnp.bfloat16),
        "tensor",
        scatter_dimension=0,
        tiled=True,
    )
    summed = lax.psum_scatter(
        lax.dot_general(
            whole, both_grads, (((0,), (0,)), ((), ())), preferred_element_type=jnp.float32
        ).astype(jnp.bfloat16),
        "replica",
        scatter_dimension=0,
        tiled=True,
    ).astype(jnp.float32)
    total = (summed * (1.0 / math.sqrt(total_tokens))).reshape(row_count, pair, units)
    keep_rows = lax.dynamic_slice_in_dim(keep, row_start, row_count, 0).astype(jnp.float32)
    weight_rows_here = lax.dynamic_slice_in_dim(weights, row_start, row_count, 0).astype(
        jnp.float32
    )
    weight_grad = (keep_rows * total).astype(jnp.bfloat16)
    new_scores = scores - math.sqrt(width) * weight_rows_here * total
    weight_grad, new_scores = (weight_grad, new_scores)
    return (token_grad, weight_grad, new_scores)


def solution(mesh):
    placed = (
        P(("replica", "tensor"), None),
        P("replica", "tensor"),
        P(None, None, "tensor"),
        P("replica", None, "tensor"),
        P(None, None, "tensor"),
    )
    return jax.shard_map(
        shards,
        mesh=mesh,
        in_specs=placed,
        out_specs=(
            P(("replica", "tensor"), None),
            P("replica", None, "tensor"),
            P("replica", None, "tensor"),
        ),
        check_vma=False,
    )
```

profile of v0, /device:TPU:0, one launch (start us, length us, event | category | flops | bytes accessed | tf_op | source)
XLA Modules:
  0.0 393.7 jit_solution(13685585745426987507)
XLA Ops:
  7.2 0.0 all-gather.2.cloned.1.call-start
  7.2 0.7 all-gather.2.cloned.1.call-update
  7.9 0.0 copy-start.2
  7.9 0.0 reduce-scatter.5.cloned.1.call-start
  8.0 36.4 %copy.14 = bf16[4096,2,896]{0,2,1:T(8,128)(2,1)} copy(bf16[4096,2,896]{2,1,0:T(2,128)(2,1)} %param.7) | data formatting | bytes 29360128 | tf_op args[2]
  44.4 0.0 copy-done.2
  44.4 13.6 %broadcast_in_dim.2 = s32[32,128,2,7,128]{1,0,4,3,2:T(8,128)} broadcast(s32[32,2,7]{0,2,1:T(8,128)S(1)} %copy.13), dimensions={0,2,3} | broadcast | bytes 29361920 | tf_op jit(solution)/shard_map/broadcast_in_dim | solution.py:14
  58.0 0.0 copy-start.1
  58.0 31.6 %reshape.16 = s32[4096,2,896]{0,2,1:T(8,128)} reshape(s32[32,128,2,7,128]{1,0,4,3,2:T(8,128)} %broadcast_in_dim.2) | data formatting | bytes 58720256 | tf_op jit(solution)/shard_map/reshape | solution.py:17
  89.6 0.0 copy-done.1
  89.6 1.1 copy.12
  90.7 19.9 %convert_multiply_fusion = bf16[4096,2,896]{0,2,1:T(8,128)(2,1)} fusion(bf16[4096,2,896]{0,2,1:T(8,128)(2,1)} %copy.14, s32[4096,2,896]{0,2,1:T(8,128)} %reshape.16), kind=kLoop, calls=%fused_computation.1 | loop fusion | flops 14680064 | bytes 58720256 | tf_op jit(solution)/shard_map/mul | solution.py:18
  110.6 0.0 all-gather.2.cloned.1.call-done
  110.6 16.1 %convolution_bitcast_fusion = f32[640,1792]{0,1:T(8,128)S(1)} fusion(bf16[4096,1792]{0,1:T(8,128)(2,1)} %bitcast.14, bf16[640,4096]{1,0:T(8,128)(2,1)} %all-gather.2.cloned.1.call-done), kind=kOutput, calls=%fused_computation.7 | convolution fusion | flops 9395240960 | bytes 24510464 | tf_op jit(solution)/shard_map/dot_general | solution.py:21
  126.7 0.0 copy-start.3
  126.7 1.1 fusion.3
  127.8 1.4 copy-done.3
  129.2 15.7 %fusion = bf16[4096,1792]{0,1:T(8,128)(2,1)} fusion(bf16[640,4096]{1,0:T(8,128)(2,1)S(1)} %copy-done.3, bf16[640,896]{0,1:T(8,128)(2,1)S(1)} %get-tuple-element.7, bf16[640,896]{0,1:T(8,128)(2,1)S(1)} %get-tuple-element.6), kind=kOutput, calls=%fused_computation.2 | convolution fusion | flops 9407168512 | bytes 22216704 | tf_op jit(solution)/shard_map/dot_general | solution.py:44
  145.0 0.0 reduce-scatter.5.cloned.1.call-update
  145.0 0.2 reduce-scatter.3.cloned.1.call-start
  145.2 14.5 %convolution_convert_fusion.1 = bf16[640,4096]{1,0:T(8,128)(2,1)} fusion(bf16[4096,1792]{0,1:T(8,128)(2,1)} %bitcast.15, bf16[640,896]{0,1:T(8,128)(2,1)S(1)} %get-tuple-element.7, bf16[640,896]{0,1:T(8,128)(2,1)S(1)} %get-tuple-element.6), kind=kOutput, calls=%fused_computation.3 | convolution fusion | flops 9402449920 | bytes 22216704 | tf_op jit(solution)/shard_map/dot_general | solution.py:36
  159.7 0.0 reduce-scatter.3.cloned.1.call-update
  159.8 6.6 %copy.16 = f32[512,2,896]{0,2,1:T(8,128)} copy(f32[512,2,896]{2,1,0:T(2,128)} %param.8) | data formatting | bytes 7340032 | tf_op args[3]
  166.3 151.2 %reduce-scatter.5.cloned.1.call-done = bf16[512,1792]{0,1:T(8,128)(2,1)} async-done(((bf16[4096,1792]{0,1:T(8,128)(2,1)}), bf16[512,1792]{0,1:T(8,128)(2,1)}) %reduce-scatter.5.cloned.1.call-update) | async-done | bytes 1835024 | tf_op jit(solution)/shard_map/reduce_scatter | solution.py:43
  317.5 0.0 copy-start
  317.5 2.2 convert_multiply_fusion.1
  319.7 0.4 copy-done
  320.1 6.0 %multiply_subtract_fusion = (f32[512,2,896]{0,2,1:T(8,128)}, bf16[512,2,896]{0,2,1:T(8,128)(2,1)S(1)}) fusion(f32[512,2,896]{0,2,1:T(8,128)S(1)} %copy-done, f32[512,2,896]{0,2,1:T(8,128)S(1)} %bitcast.16, bf16[4096,2,896]{0,2,1:T(8,128)(2,1)} %copy.14, s32[]{:T(128)S(6)} %select_n.4, s32[4096,2,896]{0,2,1:T(8,128)} %reshape.16), kind=kLoop, calls=%fused_computation.4 | loop fusion | flops 6422528 | bytes 18350084 | tf_op jit(solution)/shard_map/sub | solution.py:57
  326.1 3.6 copy.17
  329.7 6.6 %copy.18 = f32[512,2,896]{2,1,0:T(2,128)} copy(f32[512,2,896]{0,2,1:T(8,128)} %get-tuple-element.8) | data formatting | bytes 7340032
  336.3 50.9 %reduce-scatter.3.cloned.1.call-done = bf16[40,4096]{1,0:T(8,128)(2,1)} async-done(((bf16[640,4096]{1,0:T(8,128)(2,1)}), bf16[40,4096]{1,0:T(8,128)(2,1)}) %reduce-scatter.3.cloned.1.call-update) | async-done | bytes 327696 | tf_op jit(solution)/shard_map/reduce_scatter | solution.py:35
  (1 shorter events, 0.0 us)
Async XLA Ops:
  7.2 103.4 %all-gather.2.cloned.1.call-start = ((), (), s32[]{:S(2)}) async-start(), calls=%async_computation.2 | async-start | bytes 5570560 | tf_op jit(solution)/shard_map/all_gather | solution.py:20
  7.9 36.5 %copy-start.2 = (s32[32,2,7]{0,1,2:T(2,128)S(1)}, s32[32,2,7]{0,1,2:T(2,128)}, u32[]{:S(2)}) copy-start(s32[32,2,7]{0,1,2:T(2,128)} %param.9) | copy-start | bytes 5380
  7.9 309.6 %reduce-scatter.5.cloned.1.call-start = ((), (), s32[]{:S(2)}) async-start(), calls=%async_computation.4 | async-start | bytes 16515072 | tf_op jit(solution)/shard_map/reduce_scatter | solution.py:43
  58.0 31.6 %copy-start.1 = (bf16[640,896]{1,0:T(8,128)(2,1)S(1)}, bf16[640,896]{1,0:T(8,128)(2,1)}, u32[]{:S(2)}) copy-start(bf16[640,896]{1,0:T(8,128)(2,1)} %param.6) | copy-start | bytes 3440644
  126.7 2.5 copy-start.3
  145.0 242.2 %reduce-scatter.3.cloned.1.call-start = ((), (), s32[]{:S(2)}) async-start(), calls=%async_computation.3 | async-start | bytes 5570560 | tf_op jit(solution)/shard_map/reduce_scatter | solution.py:35
  317.5 2.6 copy-start
Sparse Core Ops, SparseCore 0:
  9.7 41.8 all-gather.1
  145.1 172.3 reduce-scatter.4
  320.5 66.5 reduce-scatter.2
where the time goes:
time: 396 us; the launch traced here: 394 us
  waiting for transfers between devices  203 us (51%)
  local copies, waits for them, and re-layouts  101 us (26%)
  matrix products  46.4 us (12%)
  other arithmetic  29.1 us (7%)
  between operations  13.8 us (3%)
    reduce_scatter x1, waiting for transfers between devices, shards(): lax.psum_scatter(lax.dot_general(whole, both_grads, (((0,), (0,)), ((), (...  151 us
    unnamed x14, local copies, waits for them, and re-layouts  56.1 us
    reduce_scatter x1, waiting for transfers between devices, shards(): lax.psum_scatter(lax.dot_general(both_grads, flat, (((1,), (1,)), ((), ()...  50.9 us
    reshape x1, local copies, waits for them, and re-layouts, shards(): keep = grown.reshape(width, pair, units)  31.6 us
    mul x1, other arithmetic, shards(): masked = weights * keep.astype(jnp.bfloat16)  19.9 us
    dot_general x1, matrix products, shards(): projected = jnp.dot(whole, flat, preferred_element_type=jnp.float32)  16.1 us
    dot_general x1, matrix products, shards(): lax.dot_general(whole, both_grads, (((0,), (0,)), ((), ())), preferred_el...  15.7 us
    dot_general x1, matrix products, shards(): lax.dot_general(both_grads, flat, (((1,), (1,)), ((), ())), preferred_ele...  14.5 us
  transfers between devices with their start and end apart: 3, of which 2 were waited for; matrix products, arithmetic and copies ran while one was open for 36% of the time, Pallas kernels for 0%

commit v1 on v0

v1 whole, which is shorter than its diff:
```python
import functools
import math

import jax
import jax.numpy as jnp
from jax import lax
from jax.experimental import pallas as pl
from jax.experimental.pallas import tpu as pltpu
from jax.sharding import PartitionSpec as P

TILE = 128
CHUNKS = (2, 2, 2, 1)
CORE_MAJOR = [[*range(0, 16, 2), *range(1, 16, 2)]]
STAGES = (
    (("x_hi", 0), ("rest", 0)),
    (("x_hi", 1), ("far", 0), ("token", 0)),
    (("x_hi", 2), ("near", 0), ("sum", 0), ("far", 1)),
    (("x_hi", 3), ("near", 1), ("far", 2), ("last", 0)),
    (("near", 2), ("far", 3), ("last", 1)),
    (("near", 3), ("last", 2)),
    (("last", 3),),
)
MIB = 1 << 20


def params(mib):
    return pltpu.CompilerParams(vmem_limit_bytes=mib * MIB)


SMALL = pl.CostEstimate(flops=1, bytes_accessed=1, transcendentals=0)


def over_core(v):
    return lax.ppermute(v, "tensor", [(i, i ^ 1) for i in range(16)])


def over_x_lo(v):
    return lax.ppermute(v, "tensor", [(i, i ^ 8) for i in range(16)])


def over_y(v, step):
    pairs = [(i, (i & 9) | (((i >> 1) + step) % 4) << 1) for i in range(16)]
    return lax.ppermute(v, "tensor", pairs)


def over_z(v, step):
    return lax.ppermute(v, "replica", [(i, (i + 2 * step) % 8) for i in range(8)])


def over_x_hi(v):
    return lax.ppermute(v, "replica", [(i, i ^ 1) for i in range(8)])


def after(value, *earlier):
    return lax.optimization_barrier((value, *earlier))[0]


def slot_of(where, dx, dy):
    x_lo = where[2] if dx == 0 else 1 - where[2]
    return x_lo * 4 + lax.rem(where[3] + dy, 4)


def place_body(slots, where, *refs):
    out_ref = refs[-1]
    for piece, group in zip(refs, slots):
        value = piece[...]
        for i, (dx, dy) in enumerate(group):
            out_ref[slot_of(where, dx, dy)] = value[i] if len(group) > 1 else value


def place(where, pieces, slots):
    rows, width = pieces[0].shape[-2:]
    cols = width // 2
    specs = [
        pl.BlockSpec((rows, cols), lambda i, where: (0, i))
        if piece.ndim == 2
        else pl.BlockSpec((piece.shape[0], rows, cols), lambda i, where: (0, 0, i))
        for piece in pieces
    ]
    return pl.pallas_call(
        functools.partial(place_body, slots),
        grid_spec=pltpu.PrefetchScalarGridSpec(
            num_scalar_prefetch=1,
            grid=(2,),
            in_specs=specs,
            out_specs=pl.BlockSpec((8, rows, cols), lambda i, where: (0, 0, i)),
        ),
        out_shape=jax.ShapeDtypeStruct((8, rows, width), jnp.bfloat16),
        compiler_params=params(56),
        cost_estimate=SMALL,
        name="place",
    )(where, *pieces).reshape(8 * rows, width)


def mask_body(tiles, units, begin, where, mask_ref, w_ref, *rest):
    out_ref = rest[-1]
    step = pl.program_id(0) + begin // (tiles * TILE)
    for t in range(tiles):
        rows = slice(t * TILE, (t + 1) * TILE)
        block = w_ref[rows].reshape(TILE, 2 * units * TILE)
        for j in range(units):
            for k in range(2):
                keep = mask_ref[step * tiles + t, k, j].astype(jnp.float32).astype(jnp.bfloat16)
                at = (k * units + j) * TILE
                out_ref[j, rows, k * TILE : (k + 1) * TILE] = block[:, at : at + TILE] * keep


def mask_weights(where, weights, tile_mask, begin, end, done):
    width, pair, hidden = weights.shape
    units = hidden // TILE
    rows = 256
    operands = [where, tile_mask, weights] + ([] if done is None else [done])
    return pl.pallas_call(
        functools.partial(mask_body, rows // TILE, units, begin),
        grid_spec=pltpu.PrefetchScalarGridSpec(
            num_scalar_prefetch=1,
            grid=((end - begin) // rows,),
            in_specs=[
                pl.BlockSpec(memory_space=pltpu.SMEM),
                pl.BlockSpec((rows, pair, hidden), lambda i, where: (i + begin // rows, 0, 0)),
            ]
            + ([] if done is None else [pl.BlockSpec(memory_space=pl.ANY)]),
            out_specs=pl.BlockSpec((units, rows, 256), lambda i, where: (0, i + begin // rows, 0)),
        ),
        out_shape=jax.ShapeDtypeStruct((units, width, 256), jnp.bfloat16),
        input_output_aliases={} if done is None else {3: 0},
        compiler_params=params(56),
        cost_estimate=SMALL,
        name="mask_weights",
    )(*operands)


def unit(tok, w, cot):
    both = jnp.dot(tok, w, preferred_element_type=jnp.float32)
    gate, up = both[:, :TILE], both[:, TILE:]
    sig = 1.0 / (1.0 + jnp.exp(-gate))
    upstream = cot.astype(jnp.float32)
    gate_grad = upstream * up * sig * (1.0 + gate * (1.0 - sig))
    return gate_grad.astype(jnp.bfloat16), (upstream * gate * sig).astype(jnp.bfloat16)


def first_body(where, mine_l, theirs_l, mine_r, theirs_r, w_ref, cot_ref, out_ref, tok_ref, held, sems):
    step = pl.program_id(0)
    saves = [pltpu.make_async_copy(held.at[i], tok_ref.at[i], sems.at[i]) for i in range(2)]

    @pl.when(step == 0)
    def _():
        core = where[4]
        half = mine_l.shape[1]
        left, right = pl.ds(0, half), pl.ds(half, half)
        loads = [
            pltpu.make_async_copy(mine_l, held.at[core, :, left], sems.at[0]),
            pltpu.make_async_copy(theirs_l, held.at[1 - core, :, left], sems.at[1]),
            pltpu.make_async_copy(mine_r, held.at[core, :, right], sems.at[2]),
            pltpu.make_async_copy(theirs_r, held.at[1 - core, :, right], sems.at[3]),
        ]
        for load in loads:
            load.start()
        for load in loads:
            load.wait()
        for save in saves:
            save.start()

    tok = held[...].reshape(2 * held.shape[1], held.shape[2])
    out_ref[0, :, :TILE], out_ref[0, :, TILE:] = unit(tok, w_ref[0], cot_ref[...])

    @pl.when(step == pl.num_programs(0) - 1)
    def _():
        for save in saves:
            save.wait()


def first_grads(where, parts, masked, cot, count):
    rows, width = parts[0].shape[0], masked.shape[1]
    grads, tok = pl.pallas_call(
        first_body,
        grid_spec=pltpu.PrefetchScalarGridSpec(
            num_scalar_prefetch=1,
            grid=(count,),
            in_specs=[
                *[pl.BlockSpec(memory_space=pl.ANY)] * 4,
                pl.BlockSpec((1, width, 256), lambda j, where: (j, 0, 0)),
                pl.BlockSpec((2 * rows, TILE), lambda j, where: (0, j)),
            ],
            out_specs=[
                pl.BlockSpec((1, 2 * rows, 256), lambda j, where: (j, 0, 0)),
                pl.BlockSpec(memory_space=pl.ANY),
            ],
            scratch_shapes=[pltpu.VMEM((2, rows, width), jnp.bfloat16), pltpu.SemaphoreType.DMA((4,))],
        ),
        out_shape=[
            jax.ShapeDtypeStruct((count, 2 * rows, 256), jnp.bfloat16),
            jax.ShapeDtypeStruct((2, rows, width), jnp.bfloat16),
        ],
        compiler_params=params(56),
        cost_estimate=SMALL,
        name="first_grads",
    )(where, *parts, masked, cot)
    return grads, tok.reshape(2 * rows, width)


def rest_body(counts, where, tok_ref, w_ref, cot_ref, *out_refs):
    step = pl.program_id(0)
    gate_grad, up_grad = unit(tok_ref[...], w_ref[0], cot_ref[...])
    start = 0
    for count, out_ref in zip(counts, out_refs):

        @pl.when((step >= start) & (step < start + count))
        def _(out_ref=out_ref):
            out_ref[0, :, :TILE] = gate_grad
            out_ref[0, :, TILE:] = up_grad

        start += count


def rest_grads(where, tok, masked, cot, first, counts):
    rows, width = tok.shape
    n = sum(counts)
    outs, start = [], 0
    for count in counts:
        outs.append(
            pl.BlockSpec(
                (1, rows, 256),
                lambda j, where, s=start, c=count: (jnp.clip(j - s, 0, c - 1), 0, 0),
            )
        )
        start += count
    return pl.pallas_call(
        functools.partial(rest_body, counts),
        grid_spec=pltpu.PrefetchScalarGridSpec(
            num_scalar_prefetch=1,
            grid=(n,),
            in_specs=[
                pl.BlockSpec((rows, width), lambda j, where: (0, 0)),
                pl.BlockSpec((1, width, 256), lambda j, where: (j + first, 0, 0)),
                pl.BlockSpec((rows, TILE), lambda j, where: (0, j + first)),
            ],
            out_specs=outs,
        ),
        out_shape=[jax.ShapeDtypeStruct((c, rows, 256), jnp.bfloat16) for c in counts],
        compiler_params=params(56),
        cost_estimate=SMALL,
        name="rest_grads",
    )(where, tok, masked, cot)


def outer(tok_a, tok_b, g_a, g_b, j):
    dims = (((0,), (0,)), ((), ()))
    return lax.dot_general(
        tok_a[...], g_a[j], dims, preferred_element_type=jnp.float32
    ) + lax.dot_general(tok_b[...], g_b[j], dims, preferred_element_type=jnp.float32)


def far_body(count, where, tok_a, tok_b, g_a, g_b, up_ref, down_ref):
    for j in range(count):
        part = outer(tok_a, tok_b, g_a, g_b, j).astype(jnp.bfloat16)
        up_ref[j] = part[:256]
        down_ref[j] = part[256:]


def near_body(count, where, tok_ua, tok_ub, tok_da, tok_db, g_a, g_b, got_u, got_d, up_ref, down_ref):
    for j in range(count):
        part = outer(tok_ua, tok_ub, g_a, g_b, j)
        up_ref[j, :256] = (part[:256] + got_u[j].astype(jnp.float32)).astype(jnp.bfloat16)
        up_ref[j, 256:] = part[256:].astype(jnp.bfloat16)
        part = outer(tok_da, tok_db, g_a, g_b, j)
        down_ref[j, :256] = part[:256].astype(jnp.bfloat16)
        down_ref[j, 256:] = (part[256:] + got_d[j].astype(jnp.float32)).astype(jnp.bfloat16)


def last_body(
    count, first, scale, rate, where, mask_ref, tok_a, tok_b, g_a, g_b, got_u, got_d, w_ref, s_ref, *rest
):
    wg_ref, ns_ref = rest[-2:]
    row = (where[0] * 2 + where[1]) * 4
    side = lax.broadcasted_iota(jnp.int32, (1, 2, TILE), 1)
    for j in range(count):
        total = outer(tok_a, tok_b, g_a, g_b, j)
        total = total + got_u[j].astype(jnp.float32) + got_d[j].astype(jnp.float32)
        total = total * scale
        cols = slice(j * TILE, (j + 1) * TILE)
        for t in range(4):
            rows = slice(t * TILE, (t + 1) * TILE)
            keep = jnp.where(
                side == 0, mask_ref[row + t, 0, first + j], mask_ref[row + t, 1, first + j]
            ).astype(jnp.float32)
            here = total[rows].reshape(TILE, 2, TILE)
            wg_ref[rows, :, cols] = (here * keep).astype(jnp.bfloat16)
            ns_ref[rows, :, cols] = (
                s_ref[rows, :, cols] - rate * w_ref[rows, :, cols].astype(jnp.float32) * here
            )


def tok_spec(dz):
    return pl.BlockSpec((640, 512), lambda i, where: (0, 2 * ((where[0] + dz) % 4) + where[1]))


def other_spec(dz):
    return pl.BlockSpec((640, 512), lambda i, where: (0, (where[0] + dz) % 4))


def whole(shape):
    return pl.BlockSpec(shape, lambda i, where: (0,) * len(shape))


def far_rows(where, tok, tok_other, g, g_other):
    count = g.shape[0]
    shape = (count, 256, 256)
    return pl.pallas_call(
        functools.partial(far_body, count),
        grid_spec=pltpu.PrefetchScalarGridSpec(
            num_scalar_prefetch=1,
            grid=(1,),
            in_specs=[tok_spec(2), other_spec(2), whole(g.shape), whole(g.shape)],
            out_specs=[whole(shape)] * 2,
        ),
        out_shape=[jax.ShapeDtypeStruct(shape, jnp.bfloat16)] * 2,
        compiler_params=params(56),
        cost_estimate=SMALL,
        name="far_rows",
    )(where, tok, tok_other, g, g_other)


def near_rows(where, tok, tok_other, g, g_other, got_u, got_d):
    count = g.shape[0]
    shape = (count, 512, 256)
    return pl.pallas_call(
        functools.partial(near_body, count),
        grid_spec=pltpu.PrefetchScalarGridSpec(
            num_scalar_prefetch=1,
            grid=(1,),
            in_specs=[
                tok_spec(1),
                other_spec(1),
                tok_spec(3),
                other_spec(3),
                whole(g.shape),
                whole(g.shape),
                whole(got_u.shape),
                whole(got_d.shape),
            ],
            out_specs=[whole(shape)] * 2,
        ),
        out_shape=[jax.ShapeDtypeStruct(shape, jnp.bfloat16)] * 2,
        compiler_params=params(56),
        cost_estimate=SMALL,
        name="near_rows",
    )(where, tok, tok_other, tok, tok_other, g, g_other, got_u, got_d)


def last_rows(where, tile_mask, tok, tok_other, g, g_other, got_u, got_d, weights, scores, first, done, tokens):
    count = g.shape[0]
    n = count * TILE
    at = first // count
    specs = [
        pl.BlockSpec(memory_space=pltpu.SMEM),
        tok_spec(0),
        other_spec(0),
        whole(g.shape),
        whole(g.shape),
        whole(got_u.shape),
        whole(got_d.shape),
        pl.BlockSpec((512, 2, n), lambda i, where: (where[0] * 2 + where[1], 0, at)),
        pl.BlockSpec((512, 2, n), lambda i, where: (0, 0, at)),
    ]
    out = pl.BlockSpec((512, 2, n), lambda i, where: (0, 0, at))
    operands = [where, tile_mask, tok, tok_other, g, g_other, got_u, got_d, weights, scores]
    alias = {}
    if done is not None:
        alias = {len(operands): 0, len(operands) + 1: 1}
        specs += [pl.BlockSpec(memory_space=pl.ANY)] * 2
        operands += list(done)
    return pl.pallas_call(
        functools.partial(last_body, count, first, 1.0 / math.sqrt(tokens), math.sqrt(weights.shape[0])),
        grid_spec=pltpu.PrefetchScalarGridSpec(
            num_scalar_prefetch=1, grid=(1,), in_specs=specs, out_specs=[out, out]
        ),
        out_shape=[
            jax.ShapeDtypeStruct(scores.shape, jnp.bfloat16),
            jax.ShapeDtypeStruct(scores.shape, jnp.float32),
        ],
        input_output_aliases=alias,
        compiler_params=params(56),
        cost_estimate=SMALL,
        name="last_rows",
    )(*operands)


def token_body(parts, where, *refs):
    w_ref, out_ref = refs[parts:]
    total = None
    at = 0
    for g in refs[:parts]:
        for j in range(g.shape[0]):
            term = lax.dot_general(
                g[j], w_ref[at], (((1,), (1,)), ((), ())), preferred_element_type=jnp.float32
            )
            total = term if total is None else total + term
            at += 1
    rows = out_ref.shape[1]
    for i in range(8):
        for core in range(2):
            start = (core * 8 + i) * rows
            out_ref[i * 2 + core] = total[start : start + rows].astype(jnp.bfloat16)


def token_rows(where, gs, masked):
    units, width, unused = masked.shape
    rows, cols = gs[0].shape[1], 512
    specs = [pl.BlockSpec(g.shape, lambda i, where: (0, 0, 0)) for g in gs]
    specs.append(pl.BlockSpec((units, cols, 256), lambda i, where: (0, i, 0)))
    return pl.pallas_call(
        functools.partial(token_body, len(gs)),
        grid_spec=pltpu.PrefetchScalarGridSpec(
            num_scalar_prefetch=1,
            grid=(width // cols,),
            in_specs=specs,
            out_specs=pl.BlockSpec((16, rows // 16, cols), lambda i, where: (0, 0, i)),
        ),
        out_shape=jax.ShapeDtypeStruct((16, rows // 16, width), jnp.bfloat16),
        compiler_params=params(56),
        cost_estimate=SMALL,
        name="token_rows",
    )(where, *gs, masked).reshape(rows, width)


def shards(tokens, cotangent, weights, scores, tile_mask):
    place_at, replica = lax.axis_index("tensor"), lax.axis_index("replica")
    z, x_hi = replica // 2, replica % 2
    where = jnp.stack([z, x_hi, place_at // 8, (place_at // 2) % 4, place_at % 2]).astype(jnp.int32)
    rows, width = tokens.shape
    all_tokens = rows * 16 * 8

    columns = tokens.reshape(rows, 4, 2, 512)
    sent = lax.dynamic_slice_in_dim(columns, 1 - x_hi, 1, 2).reshape(rows, 4 * 512)
    received = over_x_hi(sent)
    tok_other = lax.all_gather(received, "tensor", axis=0, tiled=True, axis_index_groups=CORE_MAJOR)

    left, right = tokens[:, : width // 2], tokens[:, width // 2 :]
    steps = (1, -1, 2)
    beside = over_x_lo(left)
    line = [right, *[over_y(right, step) for step in steps]]
    masked = mask_weights(where, weights, tile_mask, 0, 512, None)
    masked = mask_weights(after(where, received, masked), weights, tile_mask, 512, 1536, masked)
    pair = after(jnp.stack([left, beside]), masked)
    pairs = [pair, *[over_y(pair, step) for step in steps]]
    line = after(jnp.stack(line), masked)
    lines = [line, over_x_lo(line)]
    cot = cotangent.reshape(8, 2, rows, -1).transpose(1, 0, 2, 3).reshape(cotangent.shape)
    masked = mask_weights(after(where, pair, line, cot), weights, tile_mask, 1536, width, masked)
    order = (0, 3, 1, 2)
    here = after(where, masked)
    mine_l = place(here, pairs, [[(0, dy), (1, dy)] for dy in order])
    mine_r = place(here, lines, [[(dx, dy) for dy in order] for dx in range(2)])
    parts = (mine_l, over_core(mine_l), mine_r, over_core(mine_r))

    firsts = [sum(CHUNKS[:i]) for i in range(len(CHUNKS))]
    first, tok = first_grads(where, parts, masked, cot, CHUNKS[0])
    gs, others, got_far, got_near, done = [first], {}, {}, {}, None
    stage = (tok,)

    for items in STAGES:
        finished, previous = [], stage
        for kind, c in items:
            here = after(where, *stage, *previous)
            if kind == "x_hi":
                others[c] = over_x_hi(gs[c])
                finished.append(others[c])
                continue
            if c in others:
                common = (tok, tok_other, gs[c], others[c])
            if kind == "rest":
                gs += rest_grads(here, tok, masked, cot, CHUNKS[0], CHUNKS[1:])
                previous = (gs[1],)
            elif kind == "token":
                share = token_rows(here, gs, masked)
                previous = (share,)
            elif kind == "sum":
                share = after(share, *previous)
                token_grad = lax.psum_scatter(share, "tensor", scatter_dimension=0, tiled=True)
            elif kind == "far":
                up, down = far_rows(here, *common)
                got_far[c] = (over_z(up, 1), over_z(down, -1))
                previous = (up,)
                finished += got_far[c]
            elif kind == "near":
                up, down = near_rows(here, *common, *got_far[c])
                got_near[c] = (over_z(up, 1), over_z(down, -1))
                previous = (up,)
                finished += got_near[c]
            else:
                done = last_rows(
                    here, tile_mask, *common, *got_near[c], weights, scores, firsts[c], done, all_tokens
                )
                previous = (done[0],)
        stage = (*previous, *finished)
    return (token_grad, *done)


def solution(mesh):
    placed = (
        P(("replica", "tensor"), None),
        P("replica", "tensor"),
        P(None, None, "tensor"),
        P("replica", None, "tensor"),
        P(None, None, "tensor"),
    )
    return jax.shard_map(
        shards,
        mesh=mesh,
        in_specs=placed,
        out_specs=(
            P(("replica", "tensor"), None),
            P("replica", None, "tensor"),
            P("replica", None, "tensor"),
        ),
        check_vma=False,
    )
```

time: 396 us -> 234 us (0.59)
  waiting for transfers between devices: 203 us -> 23.2 us
  Pallas kernels: 0 us -> 129 us
  local copies, waits for them, and re-layouts: 101 us -> 15.5 us
  starting transfers between devices: 0.3 us -> 50.4 us
  matrix products: 46.4 us -> 0 us
  other arithmetic: 29.1 us -> 0.12 us
    reduce_scatter x2 -> x1, waiting for transfers between devices: 202 us -> 0.01 us  [shards(): lax.psum_scatter(share, 'tensor', scatter_dimension=0, tiled=True)]
    pallas_call x0 -> x20, Pallas kernels: none -> 129 us  [the longest x4 24.5 us: last_rows(): pl.pallas_call(functools.partial(last_body, count, first, 1.0 / math.sqrt...]
    ppermute x0 -> x31, starting transfers between devices: none -> 50.3 us  [the longest x16 26.1 us: over_z(): lax.ppermute(v, 'replica', [(i, (i + 2 * step) % 8) for i in range(8)])]
    dot_general x3 -> x0, matrix products: 46.4 us -> none  [the longest x1 16.1 us: shards(): projected = jnp.dot(whole, flat, preferred_element_type=jnp.float32)]
    unnamed x14 -> x70, local copies, waits for them, and re-layouts: 56.1 us -> 10.5 us
    reshape x1 -> x2, local copies, waits for them, and re-layouts: 31.6 us -> 2.31 us  [the longest x1 1.22 us: shards(): columns = tokens.reshape(rows, 4, 2, 512)]
    ppermute x0 -> x31, waiting for transfers between devices: none -> 23.2 us  [the longest x5 13 us: over_x_hi(): return lax.ppermute(v, 'replica', [(i, i ^ 1) for i in range(8)])]
    mul x2 -> x0, other arithmetic: 22.1 us -> none  [the longest x1 19.9 us: shards(): masked = weights * keep.astype(jnp.bfloat16)]
  transfers between devices with their start and end apart: 3 -> 33, of which waited for: 2 -> 6; matrix products, arithmetic and copies ran while one was open for 36% -> 2% of each run, Pallas kernels for 0% -> 53%
where the time goes in v1:
time: 234 us; the launch traced here: 233 us
  Pallas kernels  129 us (55%)
  starting transfers between devices  50.4 us (22%)
  waiting for transfers between devices  23.2 us (10%)
  local copies, waits for them, and re-layouts  15.5 us (7%)
  between operations  14.5 us (6%)
    ppermute x16, starting transfers between devices, over_z(): lax.ppermute(v, 'replica', [(i, (i + 2 * step) % 8) for i in range(8)])  26.1 us
    pallas_call x4, Pallas kernels, last_rows(): pl.pallas_call(functools.partial(last_body, count, first, 1.0 / math.sqrt...  24.5 us
    pallas_call x3, Pallas kernels, mask_weights(): pl.pallas_call(functools.partial(mask_body, rows // TILE, units, begin),...  23 us
    pallas_call x4, Pallas kernels, near_rows(): pl.pallas_call(functools.partial(near_body, count), grid_spec=pltpu.Prefe...  21.7 us
    pallas_call x1, Pallas kernels, token_rows(): pl.pallas_call(functools.partial(token_body, len(gs)), grid_spec=pltpu.Pr...  16.1 us
    pallas_call x4, Pallas kernels, far_rows(): pl.pallas_call(functools.partial(far_body, count), grid_spec=pltpu.Prefet...  15.8 us
    pallas_call x1, Pallas kernels, rest_grads(): pl.pallas_call(functools.partial(rest_body, counts), grid_spec=pltpu.Pref...  13.1 us
    ppermute x5, waiting for transfers between devices, over_x_hi(): return lax.ppermute(v, 'replica', [(i, i ^ 1) for i in range(8)])  13 us
  transfers between devices with their start and end apart: 33, of which 6 were waited for; matrix products, arithmetic and copies ran while one was open for 2% of the time, Pallas kernels for 53%

profile of v1, /device:TPU:0, one launch (start us, length us, event | category | flops | bytes accessed | tf_op | source)
XLA Modules:
  0.0 232.8 jit_solution(13873218965107875961)
XLA Ops:
  9.5 3.2 %collective-permute-start.1 = (bf16[40,2048]{1,0:T(8,128)(2,1)S(1)}, bf16[40,2048]{1,0:T(8,128)(2,1)S(1)}, u32[]{:S(2)}, u32[]{:S(2)}) collective-permute-start(bf16[40,2048]{1,0:T(8,128)(2,1)S(1)} %bitcast.53), channel_id=1, source_target_pairs={{0,1},{1,0},{2,3},{3,2},{4,5},{5,4},{6,7},{7,6},{8,9},{9,8},{10,11... | collective-permute-start | bytes 491528 | tf_op jit(solution)/shard_map/ppermute | solution.py:51
  12.7 4.2 %collective-permute-done.1 = bf16[40,2048]{1,0:T(8,128)(2,1)S(1)} collective-permute-done((bf16[40,2048]{1,0:T(8,128)(2,1)S(1)}, bf16[40,2048]{1,0:T(8,128)(2,1)S(1)}, u32[]{:S(2)}, u32[]{:S(2)}) %collective-permute-start.1) | collective-permute-done | bytes 163872 | tf_op jit(solution)/shard_map/ppermute | solution.py:51
  18.7 3.5 %collective-permute-start.4 = (bf16[40,2048]{1,0:T(8,128)(2,1)S(1)}, bf16[40,2048]{1,0:T(8,128)(2,1)S(1)}, u32[]{:S(2)}, u32[]{:S(2)}) collective-permute-start(bf16[40,2048]{1,0:T(8,128)(2,1)S(1)} %get-tuple-element.104), channel_id=1, source_target_pairs={{0,32},{8,40},{16,48},{24,56},{32,0},{40,8},{48,16},{56,24},{64,96... | collective-permute-start | bytes 491528 | tf_op jit(solution)/shard_map/ppermute | solution.py:43
  28.9 3.8 %mask_weights.3.rest_0_ = bf16[7,4096,256]{2,1,0:T(8,128)(2,1)} custom-call(s32[5]{0:T(128)} %stack.47.where, s32[32,2,7]{2,1,0:T(2,128)} %copy.17.mask_ref, bf16[4096,2,896]{2,1,0:T(2,128)(2,1)} %w_ref.13), custom_call_target="tpu_custom_call" | custom-call | flops 1 | bytes 1 | tf_op jit(solution)/shard_map/mask_weights/pallas_call | solution.py:113
  32.9 6.3 %mask_weights.4.rest_0_ = bf16[7,4096,256]{2,1,0:T(8,128)(2,1)} custom-call(s32[5]{0:T(128)} %stack.47.where, s32[32,2,7]{2,1,0:T(2,128)} %copy.17.mask_ref, bf16[4096,2,896]{2,1,0:T(2,128)(2,1)} %w_ref.13, bf16[7,4096,256]{2,1,0:T(8,128)(2,1)} %mask_weights.3.rest_0_), custom_call_target="tpu_custom_call", output_to_operand_aliasing={{}: (3, {})} | custom-call | flops 1 | bytes 1 | tf_op jit(solution)/shard_map/mask_weights/pallas_call | solution.py:113
  39.8 3.2 %collective-permute-start.6 = (bf16[2,40,2048]{2,1,0:T(8,128)(2,1)S(1)}, bf16[2,40,2048]{2,1,0:T(8,128)(2,1)S(1)}, u32[]{:S(2)}, u32[]{:S(2)}) collective-permute-start(bf16[2,40,2048]{2,1,0:T(8,128)(2,1)S(1)} %pad_maximum_fusion.1.refs_0_), channel_id=1, source_target_pairs={{0,48},{8,56},{16,0},{24,8},{32,16},{40,24},{48,32},{56,40},{64,11... | collective-permute-start | bytes 983048 | tf_op jit(solution)/shard_map/ppermute | solution.py:43
  44.2 13.0 %mask_weights.5.w_ref.refs_4_ = bf16[7,4096,256]{2,1,0:T(8,128)(2,1)} custom-call(s32[5]{0:T(128)} %stack.47.where, s32[32,2,7]{2,1,0:T(2,128)} %copy.17.mask_ref, bf16[4096,2,896]{2,1,0:T(2,128)(2,1)} %w_ref.13, bf16[7,4096,256]{2,1,0:T(8,128)(2,1)} %mask_weights.4.rest_0_), custom_call_target="tpu_custom_call", output_to_operand_aliasing={{}: (3, {})} | custom-call | flops 1 | bytes 1 | tf_op jit(solution)/shard_map/mask_weights/pallas_call | solution.py:113
  57.1 5.4 %collective-permute-done.7.refs_3_ = bf16[2,40,2048]{2,1,0:T(8,128)(2,1)S(1)} collective-permute-done((bf16[2,40,2048]{2,1,0:T(8,128)(2,1)S(1)}, bf16[2,40,2048]{2,1,0:T(8,128)(2,1)S(1)}, u32[]{:S(2)}, u32[]{:S(2)}) %collective-permute-start.7) | collective-permute-done | bytes 327712 | tf_op jit(solution)/shard_map/ppermute | solution.py:43
  63.3 3.0 %place.2 = bf16[8,40,2048]{2,1,0:T(8,128)(2,1)} custom-call(s32[5]{0:T(128)} %stack.47.where, bf16[2,40,2048]{2,1,0:T(8,128)(2,1)} %copy-done.9, bf16[2,40,2048]{2,1,0:T(8,128)(2,1)} %copy-done.18, bf16[2,40,2048]{2,1,0:T(8,128)(2,1)} %copy-done.19, bf16[2,40,2048]{2,1,0:T(8,128)(2,1)} %copy-done.20), custom_call_target="tpu_custom_call" | custom-call | flops 1 | bytes 1 | tf_op jit(solution)/shard_map/place/pallas_call | solution.py:80
  74.4 9.1 %first_grads.1 = (bf16[2,640,256]{2,1,0:T(8,128)(2,1)}, bf16[2,320,4096]{2,1,0:T(8,128)(2,1)}) custom-call(s32[5]{0:T(128)} %stack.47.where, bf16[320,2048]{1,0:T(8,128)(2,1)} %bitcast.44, bf16[320,2048]{1,0:T(8,128)(2,1)} %copy-done.7, bf16[320,2048]{1,0:T(8,128)(2,1)} %bitcast.46, bf16[320,2048]{1,0:T(8,128)(2,1)} %copy-done.8, ...), custom_call_target="tpu_custom_call" | custom-call | flops 1 | bytes 1 | tf_op jit(solution)/shard_map/first_grads/pallas_call | solution.py:175
  86.4 13.1 %rest_grads.1 = (bf16[2,640,256]{2,1,0:T(8,128)(2,1)}, bf16[2,640,256]{2,1,0:T(8,128)(2,1)}, bf16[1,640,256]{2,1,0:T(8,128)(2,1)}) custom-call(s32[5]{0:T(128)} %stack.47.where, bf16[640,4096]{1,0:T(8,128)(2,1)} %bitcast.23, bf16[7,4096,256]{2,1,0:T(8,128)(2,1)} %mask_weights.5.w_ref.refs_4_, bf16[640,896]{1,0:T(8,128)(2,1)} %bitcast.42), custom_call_target="tpu_custom_call" | custom-call | flops 1 | bytes 1 | tf_op jit(solution)/shard_map/rest_grads/pallas_call | solution.py:228
  103.2 4.1 %far_rows.4 = (bf16[2,256,256]{2,1,0:T(8,128)(2,1)}, bf16[2,256,256]{2,1,0:T(8,128)(2,1)}) custom-call(s32[5]{0:T(128)} %stack.47.where, bf16[640,4096]{1,0:T(8,128)(2,1)} %bitcast.24, bf16[640,2048]{1,0:T(8,128)(2,1)} %all-gather.2.cloned.1.call-done.tok_b.tok_ub.tok_db, bf16[2,640,256]{2,1,0:T(8,128)(2,1)} %get-tuple-element.60.g_a.refs_0_, ...), custom_call_target="tpu_custom_call" | custom-call | flops 1 | bytes 1 | tf_op jit(solution)/shard_map/far_rows/pallas_call | solution.py:309
  110.5 16.1 %token_rows.1 = bf16[16,40,4096]{2,1,0:T(8,128)(2,1)} custom-call(s32[5]{0:T(128)} %stack.47.where, bf16[2,640,256]{2,1,0:T(8,128)(2,1)} %get-tuple-element.60.g_a.refs_0_, bf16[2,640,256]{2,1,0:T(8,128)(2,1)} %get-tuple-element.59.refs_1_.g_a, bf16[2,640,256]{2,1,0:T(8,128)(2,1)} %get-tuple-element.64.refs_2_.g_a, ...), custom_call_target="tpu_custom_call" | custom-call | flops 1 | bytes 1 | tf_op jit(solution)/shard_map/token_rows/pallas_call | solution.py:412
  127.5 5.7 %near_rows.4 = (bf16[2,512,256]{2,1,0:T(8,128)(2,1)}, bf16[2,512,256]{2,1,0:T(8,128)(2,1)}) custom-call(s32[5]{0:T(128)} %stack.47.where, bf16[640,4096]{1,0:T(8,128)(2,1)} %bitcast.25, bf16[640,2048]{1,0:T(8,128)(2,1)} %all-gather.2.cloned.1.call-done.tok_b.tok_ub.tok_db, bf16[640,4096]{1,0:T(8,128)(2,1)} %bitcast.26, ...), custom_call_target="tpu_custom_call" | custom-call | flops 1 | bytes 1 | tf_op jit(solution)/shard_map/near_rows/pallas_call | solution.py:327
  134.3 3.1 %collective-permute-start.15 = (bf16[2,640,256]{2,1,0:T(8,128)(2,1)S(1)}, bf16[2,640,256]{2,1,0:T(8,128)(2,1)S(1)}, u32[]{:S(2)}, u32[]{:S(2)}) collective-permute-start(bf16[2,640,256]{2,1,0:T(8,128)(2,1)S(1)} %copy-done), channel_id=1, source_target_pairs={{0,1},{1,0},{2,3},{3,2},{4,5},{5,4},{6,7},{7,6},{8,9},{9,8},{10,11... | collective-permute-start | bytes 1966088 | tf_op jit(solution)/shard_map/ppermute | solution.py:51
  140.6 4.1 %far_rows.5 = (bf16[2,256,256]{2,1,0:T(8,128)(2,1)}, bf16[2,256,256]{2,1,0:T(8,128)(2,1)}) custom-call(s32[5]{0:T(128)} %stack.47.where, bf16[640,4096]{1,0:T(8,128)(2,1)} %bitcast.27, bf16[640,2048]{1,0:T(8,128)(2,1)} %all-gather.2.cloned.1.call-done.tok_b.tok_ub.tok_db, bf16[2,640,256]{2,1,0:T(8,128)(2,1)} %get-tuple-element.59.refs_1_.g_a, ...), custom_call_target="tpu_custom_call" | custom-call | flops 1 | bytes 1 | tf_op jit(solution)/shard_map/far_rows/pallas_call | solution.py:309
  144.8 3.2 %collective-permute-start.19 = (bf16[2,256,256]{2,1,0:T(8,128)(2,1)}, bf16[2,256,256]{2,1,0:T(8,128)(2,1)S(1)}, u32[]{:S(2)}, u32[]{:S(2)}) collective-permute-start(bf16[2,256,256]{2,1,0:T(8,128)(2,1)} %get-tuple-element.73), channel_id=1, source_target_pairs={{0,6},{1,7},{2,0},{3,1},{4,2},{5,3},{6,4},{7,5},{8,14},{9,15},{10,... | collective-permute-start | bytes 786440 | tf_op jit(solution)/shard_map/ppermute | solution.py:47
  148.0 6.7 %collective-permute-done.15.g_b = bf16[2,640,256]{2,1,0:T(8,128)(2,1)S(1)} collective-permute-done((bf16[2,640,256]{2,1,0:T(8,128)(2,1)S(1)}, bf16[2,640,256]{2,1,0:T(8,128)(2,1)S(1)}, u32[]{:S(2)}, u32[]{:S(2)}) %collective-permute-start.15) | collective-permute-done | bytes 655392 | tf_op jit(solution)/shard_map/ppermute | solution.py:51
  157.4 5.7 %near_rows.5 = (bf16[2,512,256]{2,1,0:T(8,128)(2,1)}, bf16[2,512,256]{2,1,0:T(8,128)(2,1)}) custom-call(s32[5]{0:T(128)} %stack.47.where, bf16[640,4096]{1,0:T(8,128)(2,1)} %bitcast.28, bf16[640,2048]{1,0:T(8,128)(2,1)} %all-gather.2.cloned.1.call-done.tok_b.tok_ub.tok_db, bf16[640,4096]{1,0:T(8,128)(2,1)} %bitcast.29, ...), custom_call_target="tpu_custom_call" | custom-call | flops 1 | bytes 1 | tf_op jit(solution)/shard_map/near_rows/pallas_call | solution.py:327
  163.4 3.0 %collective-permute-start.22 = (bf16[2,512,256]{2,1,0:T(8,128)(2,1)}, bf16[2,512,256]{2,1,0:T(8,128)(2,1)S(1)}, u32[]{:S(2)}, u32[]{:S(2)}) collective-permute-start(bf16[2,512,256]{2,1,0:T(8,128)(2,1)} %get-tuple-element.80), channel_id=1, source_target_pairs={{0,6},{1,7},{2,0},{3,1},{4,2},{5,3},{6,4},{7,5},{8,14},{9,15},{10,... | collective-permute-start | bytes 1572872 | tf_op jit(solution)/shard_map/ppermute | solution.py:47
  168.2 4.1 %far_rows.6 = (bf16[2,256,256]{2,1,0:T(8,128)(2,1)}, bf16[2,256,256]{2,1,0:T(8,128)(2,1)}) custom-call(s32[5]{0:T(128)} %stack.47.where, bf16[640,4096]{1,0:T(8,128)(2,1)} %bitcast.30, bf16[640,2048]{1,0:T(8,128)(2,1)} %all-gather.2.cloned.1.call-done.tok_b.tok_ub.tok_db, bf16[2,640,256]{2,1,0:T(8,128)(2,1)} %get-tuple-element.64.refs_2_.g_a, ...), custom_call_target="tpu_custom_call" | custom-call | flops 1 | bytes 1 | tf_op jit(solution)/shard_map/far_rows/pallas_call | solution.py:309
  172.3 3.2 %collective-permute-start.24 = (bf16[2,256,256]{2,1,0:T(8,128)(2,1)}, bf16[2,256,256]{2,1,0:T(8,128)(2,1)S(1)}, u32[]{:S(2)}, u32[]{:S(2)}) collective-permute-start(bf16[2,256,256]{2,1,0:T(8,128)(2,1)} %get-tuple-element.81), channel_id=1, source_target_pairs={{0,6},{1,7},{2,0},{3,1},{4,2},{5,3},{6,4},{7,5},{8,14},{9,15},{10,... | collective-permute-start | bytes 786440 | tf_op jit(solution)/shard_map/ppermute | solution.py:47
  175.6 6.6 %last_rows.4 = (bf16[512,2,896]{2,1,0:T(2,128)(2,1)}, f32[512,2,896]{2,1,0:T(2,128)}) custom-call(s32[5]{0:T(128)} %stack.47.where, s32[32,2,7]{2,1,0:T(2,128)} %copy.17.mask_ref, bf16[640,4096]{1,0:T(8,128)(2,1)} %bitcast.31, bf16[640,2048]{1,0:T(8,128)(2,1)} %all-gather.2.cloned.1.call-done.tok_b.tok_ub.tok_db, ...), custom_call_target="tpu_custom_call" | custom-call | flops 1 | bytes 1 | tf_op jit(solution)/shard_map/last_rows/pallas_call | solution.py:373
  183.1 5.8 %near_rows.6 = (bf16[2,512,256]{2,1,0:T(8,128)(2,1)}, bf16[2,512,256]{2,1,0:T(8,128)(2,1)}) custom-call(s32[5]{0:T(128)} %stack.47.where, bf16[640,4096]{1,0:T(8,128)(2,1)} %bitcast.32, bf16[640,2048]{1,0:T(8,128)(2,1)} %all-gather.2.cloned.1.call-done.tok_b.tok_ub.tok_db, bf16[640,4096]{1,0:T(8,128)(2,1)} %bitcast.33, ...), custom_call_target="tpu_custom_call" | custom-call | flops 1 | bytes 1 | tf_op jit(solution)/shard_map/near_rows/pallas_call | solution.py:327
  189.1 3.1 %collective-permute-start.26 = (bf16[2,512,256]{2,1,0:T(8,128)(2,1)}, bf16[2,512,256]{2,1,0:T(8,128)(2,1)S(1)}, u32[]{:S(2)}, u32[]{:S(2)}) collective-permute-start(bf16[2,512,256]{2,1,0:T(8,128)(2,1)} %get-tuple-element.89), channel_id=1, source_target_pairs={{0,6},{1,7},{2,0},{3,1},{4,2},{5,3},{6,4},{7,5},{8,14},{9,15},{10,... | collective-permute-start | bytes 1572872 | tf_op jit(solution)/shard_map/ppermute | solution.py:47
  192.1 3.5 %far_rows.7 = (bf16[1,256,256]{2,1,0:T(8,128)(2,1)}, bf16[1,256,256]{2,1,0:T(8,128)(2,1)}) custom-call(s32[5]{0:T(128)} %stack.47.where, bf16[640,4096]{1,0:T(8,128)(2,1)} %bitcast.34, bf16[640,2048]{1,0:T(8,128)(2,1)} %all-gather.2.cloned.1.call-done.tok_b.tok_ub.tok_db, bf16[1,640,256]{2,1,0:T(8,128)(2,1)} %get-tuple-element.65.refs_3_.g_a, ...), custom_call_target="tpu_custom_call" | custom-call | flops 1 | bytes 1 | tf_op jit(solution)/shard_map/far_rows/pallas_call | solution.py:309
  195.6 3.2 %collective-permute-start.28 = (bf16[1,256,256]{2,1,0:T(8,128)(2,1)}, bf16[1,256,256]{2,1,0:T(8,128)(2,1)S(1)}, u32[]{:S(2)}, u32[]{:S(2)}) collective-permute-start(bf16[1,256,256]{2,1,0:T(8,128)(2,1)} %get-tuple-element.90), channel_id=1, source_target_pairs={{0,6},{1,7},{2,0},{3,1},{4,2},{5,3},{6,4},{7,5},{8,14},{9,15},{10,... | collective-permute-start | bytes 393224 | tf_op jit(solution)/shard_map/ppermute | solution.py:47
  198.8 6.6 %last_rows.5 = (bf16[512,2,896]{2,1,0:T(2,128)(2,1)}, f32[512,2,896]{2,1,0:T(2,128)}) custom-call(s32[5]{0:T(128)} %stack.47.where, s32[32,2,7]{2,1,0:T(2,128)} %copy.17.mask_ref, bf16[640,4096]{1,0:T(8,128)(2,1)} %bitcast.35, bf16[640,2048]{1,0:T(8,128)(2,1)} %all-gather.2.cloned.1.call-done.tok_b.tok_ub.tok_db, ...), custom_call_target="tpu_custom_call", output_to_operand_aliasing={{0}: (10, {}), {1}: (11, {})} | custom-call | flops 1 | bytes 1 | tf_op jit(solution)/shard_map/last_rows/pallas_call | solution.py:373
  206.2 4.5 %near_rows.7 = (bf16[1,512,256]{2,1,0:T(8,128)(2,1)}, bf16[1,512,256]{2,1,0:T(8,128)(2,1)}) custom-call(s32[5]{0:T(128)} %stack.47.where, bf16[640,4096]{1,0:T(8,128)(2,1)} %bitcast.36, bf16[640,2048]{1,0:T(8,128)(2,1)} %all-gather.2.cloned.1.call-done.tok_b.tok_ub.tok_db, bf16[640,4096]{1,0:T(8,128)(2,1)} %bitcast.37, ...), custom_call_target="tpu_custom_call" | custom-call | flops 1 | bytes 1 | tf_op jit(solution)/shard_map/near_rows/pallas_call | solution.py:327
  210.7 3.2 %collective-permute-start.30 = (bf16[1,512,256]{2,1,0:T(8,128)(2,1)}, bf16[1,512,256]{2,1,0:T(8,128)(2,1)S(1)}, u32[]{:S(2)}, u32[]{:S(2)}) collective-permute-start(bf16[1,512,256]{2,1,0:T(8,128)(2,1)} %get-tuple-element.96), channel_id=1, source_target_pairs={{0,6},{1,7},{2,0},{3,1},{4,2},{5,3},{6,4},{7,5},{8,14},{9,15},{10,... | collective-permute-start | bytes 786440 | tf_op jit(solution)/shard_map/ppermute | solution.py:47
  213.9 6.6 %last_rows.6 = (bf16[512,2,896]{2,1,0:T(2,128)(2,1)}, f32[512,2,896]{2,1,0:T(2,128)}) custom-call(s32[5]{0:T(128)} %stack.47.where, s32[32,2,7]{2,1,0:T(2,128)} %copy.17.mask_ref, bf16[640,4096]{1,0:T(8,128)(2,1)} %bitcast.38, bf16[640,2048]{1,0:T(8,128)(2,1)} %all-gather.2.cloned.1.call-done.tok_b.tok_ub.tok_db, ...), custom_call_target="tpu_custom_call", output_to_operand_aliasing={{0}: (10, {}), {1}: (11, {})} | custom-call | flops 1 | bytes 1 | tf_op jit(solution)/shard_map/last_rows/pallas_call | solution.py:373
  221.4 4.6 %last_rows.7 = (bf16[512,2,896]{2,1,0:T(2,128)(2,1)}, f32[512,2,896]{2,1,0:T(2,128)}) custom-call(s32[5]{0:T(128)} %stack.47.where, s32[32,2,7]{2,1,0:T(2,128)} %copy.17.mask_ref, bf16[640,4096]{1,0:T(8,128)(2,1)} %bitcast.39, bf16[640,2048]{1,0:T(8,128)(2,1)} %all-gather.2.cloned.1.call-done.tok_b.tok_ub.tok_db, ...), custom_call_target="tpu_custom_call", output_to_operand_aliasing={{0}: (10, {}), {1}: (11, {})} | custom-call | flops 1 | bytes 1 | tf_op jit(solution)/shard_map/last_rows/pallas_call | solution.py:373
  (133 shorter events, 43.8 us)
Async XLA Ops:
  7.2 95.2 %all-gather.2.cloned.1.call-start = ((), (), s32[]{:S(2)}) async-start(), calls=%async_computation.1 | async-start | bytes 2785280 | tf_op jit(solution)/shard_map/all_gather | solution.py:437
  9.5 7.4 %collective-permute-start.1 = (bf16[40,2048]{1,0:T(8,128)(2,1)S(1)}, bf16[40,2048]{1,0:T(8,128)(2,1)S(1)}, u32[]{:S(2)}, u32[]{:S(2)}) collective-permute-start(bf16[40,2048]{1,0:T(8,128)(2,1)S(1)} %bitcast.53), channel_id=1, source_target_pairs={{0,1},{1,0},{2,3},{3,2},{4,5},{5,4},{6,7},{7,6},{8,9},{9,8},{10,11... | collective-permute-start | bytes 491528 | tf_op jit(solution)/shard_map/ppermute | solution.py:51
  17.6 208.4 %reduce-scatter.2.cloned.1.call-start = ((), (), s32[]{:S(2)}) async-start(), calls=%async_computation.2 | async-start | bytes 5570560 | tf_op jit(solution)/shard_map/reduce_scatter | solution.py:480
  18.7 14.0 %collective-permute-start.4 = (bf16[40,2048]{1,0:T(8,128)(2,1)S(1)}, bf16[40,2048]{1,0:T(8,128)(2,1)S(1)}, u32[]{:S(2)}, u32[]{:S(2)}) collective-permute-start(bf16[40,2048]{1,0:T(8,128)(2,1)S(1)} %get-tuple-element.104), channel_id=1, source_target_pairs={{0,32},{8,40},{16,48},{24,56},{32,0},{40,8},{48,16},{56,24},{64,96... | collective-permute-start | bytes 491528 | tf_op jit(solution)/shard_map/ppermute | solution.py:43
  22.2 10.5 %collective-permute-start.2 = (bf16[40,2048]{1,0:T(8,128)(2,1)S(1)}, bf16[40,2048]{1,0:T(8,128)(2,1)S(1)}, u32[]{:S(2)}, u32[]{:S(2)}) collective-permute-start(bf16[40,2048]{1,0:T(8,128)(2,1)S(1)} %get-tuple-element.104), channel_id=1, source_target_pairs={{0,16},{8,24},{16,32},{24,40},{32,48},{40,56},{48,0},{56,8},{64,80... | collective-permute-start | bytes 491528 | tf_op jit(solution)/shard_map/ppermute | solution.py:43
  22.9 9.9 %collective-permute-start.3 = (bf16[40,2048]{1,0:T(8,128)(2,1)S(1)}, bf16[40,2048]{1,0:T(8,128)(2,1)S(1)}, u32[]{:S(2)}, u32[]{:S(2)}) collective-permute-start(bf16[40,2048]{1,0:T(8,128)(2,1)S(1)} %get-tuple-element.104), channel_id=1, source_target_pairs={{0,48},{8,56},{16,0},{24,8},{32,16},{40,24},{48,32},{56,40},{64,11... | collective-permute-start | bytes 491528 | tf_op jit(solution)/shard_map/ppermute | solution.py:43
  25.5 14.2 %collective-permute-start = (bf16[40,2048]{1,0:T(8,128)(2,1)S(1)}, bf16[40,2048]{1,0:T(8,128)(2,1)S(1)}, u32[]{:S(2)}, u32[]{:S(2)}) collective-permute-start(bf16[40,2048]{1,0:T(8,128)(2,1)S(1)} %get-tuple-element.103), channel_id=1, source_target_pairs={{0,64},{8,72},{16,80},{24,88},{32,96},{40,104},{48,112},{56,120},{... | collective-permute-start | bytes 491528 | tf_op jit(solution)/shard_map/ppermute | solution.py:38
  39.2 27.1 %collective-permute-start.9 = (bf16[4,40,2048]{2,1,0:T(8,128)(2,1)S(1)}, bf16[4,40,2048]{2,1,0:T(8,128)(2,1)S(1)}, u32[]{:S(2)}, u32[]{:S(2)}) collective-permute-start(bf16[4,40,2048]{2,1,0:T(8,128)(2,1)S(1)} %pad_maximum_fusion.refs_0_), channel_id=1, source_target_pairs={{0,64},{8,72},{16,80},{24,88},{32,96},{40,104},{48,112},{56,120},{... | collective-permute-start | bytes 1966088 | tf_op jit(solution)/shard_map/ppermute | solution.py:38
  39.8 17.4 %collective-permute-start.5 = (bf16[2,40,2048]{2,1,0:T(8,128)(2,1)S(1)}, bf16[2,40,2048]{2,1,0:T(8,128)(2,1)S(1)}, u32[]{:S(2)}, u32[]{:S(2)}) collective-permute-start(bf16[2,40,2048]{2,1,0:T(8,128)(2,1)S(1)} %pad_maximum_fusion.1.refs_0_), channel_id=1, source_target_pairs={{0,16},{8,24},{16,32},{24,40},{32,48},{40,56},{48,0},{56,8},{64,80... | collective-permute-start | bytes 983048 | tf_op jit(solution)/shard_map/ppermute | solution.py:43
  39.8 17.3 %collective-permute-start.6 = (bf16[2,40,2048]{2,1,0:T(8,128)(2,1)S(1)}, bf16[2,40,2048]{2,1,0:T(8,128)(2,1)S(1)}, u32[]{:S(2)}, u32[]{:S(2)}) collective-permute-start(bf16[2,40,2048]{2,1,0:T(8,128)(2,1)S(1)} %pad_maximum_fusion.1.refs_0_), channel_id=1, source_target_pairs={{0,48},{8,56},{16,0},{24,8},{32,16},{40,24},{48,32},{56,40},{64,11... | collective-permute-start | bytes 983048 | tf_op jit(solution)/shard_map/ppermute | solution.py:43
  43.1 19.5 %collective-permute-start.7 = (bf16[2,40,2048]{2,1,0:T(8,128)(2,1)S(1)}, bf16[2,40,2048]{2,1,0:T(8,128)(2,1)S(1)}, u32[]{:S(2)}, u32[]{:S(2)}) collective-permute-start(bf16[2,40,2048]{2,1,0:T(8,128)(2,1)S(1)} %pad_maximum_fusion.1.refs_0_), channel_id=1, source_target_pairs={{0,32},{8,40},{16,48},{24,56},{32,0},{40,8},{48,16},{56,24},{64,96... | collective-permute-start | bytes 983048 | tf_op jit(solution)/shard_map/ppermute | solution.py:43
  66.3 4.2 %collective-permute-start.8 = (bf16[320,2048]{1,0:T(8,128)(2,1)}, bf16[320,2048]{1,0:T(8,128)(2,1)S(1)}, u32[]{:S(2)}, u32[]{:S(2)}) collective-permute-start(bf16[320,2048]{1,0:T(8,128)(2,1)} %bitcast.43), channel_id=1, source_target_pairs={{0,8},{8,0},{16,24},{24,16},{32,40},{40,32},{48,56},{56,48},{64,72... | collective-permute-start | bytes 3932168 | tf_op jit(solution)/shard_map/ppermute | solution.py:34
  83.5 18.8 %collective-permute-start.11 = (bf16[2,640,256]{2,1,0:T(8,128)(2,1)}, bf16[2,640,256]{2,1,0:T(8,128)(2,1)S(1)}, u32[]{:S(2)}, u32[]{:S(2)}) collective-permute-start(bf16[2,640,256]{2,1,0:T(8,128)(2,1)} %get-tuple-element.60.g_a.refs_0_), channel_id=1, source_target_pairs={{0,1},{1,0},{2,3},{3,2},{4,5},{5,4},{6,7},{7,6},{8,9},{9,8},{10,11... | collective-permute-start | bytes 1966088 | tf_op jit(solution)/shard_map/ppermute | solution.py:51
  99.5 27.2 %collective-permute-start.12 = (bf16[2,640,256]{2,1,0:T(8,128)(2,1)}, bf16[2,640,256]{2,1,0:T(8,128)(2,1)S(1)}, u32[]{:S(2)}, u32[]{:S(2)}) collective-permute-start(bf16[2,640,256]{2,1,0:T(8,128)(2,1)} %get-tuple-element.59.refs_1_.g_a), channel_id=1, source_target_pairs={{0,1},{1,0},{2,3},{3,2},{4,5},{5,4},{6,7},{7,6},{8,9},{9,8},{10,11... | collective-permute-start | bytes 1966088 | tf_op jit(solution)/shard_map/ppermute | solution.py:51
  107.3 19.4 %collective-permute-start.13 = (bf16[2,256,256]{2,1,0:T(8,128)(2,1)}, bf16[2,256,256]{2,1,0:T(8,128)(2,1)S(1)}, u32[]{:S(2)}, u32[]{:S(2)}) collective-permute-start(bf16[2,256,256]{2,1,0:T(8,128)(2,1)} %get-tuple-element.62), channel_id=1, source_target_pairs={{0,2},{1,3},{2,4},{3,5},{4,6},{5,7},{6,0},{7,1},{8,10},{9,11},{10,... | collective-permute-start | bytes 786440 | tf_op jit(solution)/shard_map/ppermute | solution.py:47
  108.8 17.8 %collective-permute-start.14 = (bf16[2,256,256]{2,1,0:T(8,128)(2,1)}, bf16[2,256,256]{2,1,0:T(8,128)(2,1)S(1)}, u32[]{:S(2)}, u32[]{:S(2)}) collective-permute-start(bf16[2,256,256]{2,1,0:T(8,128)(2,1)} %get-tuple-element.66), channel_id=1, source_target_pairs={{0,6},{1,7},{2,0},{3,1},{4,2},{5,3},{6,4},{7,5},{8,14},{9,15},{10,... | collective-permute-start | bytes 786440 | tf_op jit(solution)/shard_map/ppermute | solution.py:47
  134.3 20.4 %collective-permute-start.15 = (bf16[2,640,256]{2,1,0:T(8,128)(2,1)S(1)}, bf16[2,640,256]{2,1,0:T(8,128)(2,1)S(1)}, u32[]{:S(2)}, u32[]{:S(2)}) collective-permute-start(bf16[2,640,256]{2,1,0:T(8,128)(2,1)S(1)} %copy-done), channel_id=1, source_target_pairs={{0,1},{1,0},{2,3},{3,2},{4,5},{5,4},{6,7},{7,6},{8,9},{9,8},{10,11... | collective-permute-start | bytes 1966088 | tf_op jit(solution)/shard_map/ppermute | solution.py:51
  137.4 19.2 %collective-permute-start.16 = (bf16[2,512,256]{2,1,0:T(8,128)(2,1)S(1)}, bf16[2,512,256]{2,1,0:T(8,128)(2,1)S(1)}, u32[]{:S(2)}, u32[]{:S(2)}) collective-permute-start(bf16[2,512,256]{2,1,0:T(8,128)(2,1)S(1)} %copy-done.33), channel_id=1, source_target_pairs={{0,2},{1,3},{2,4},{3,5},{4,6},{5,7},{6,0},{7,1},{8,10},{9,11},{10,... | collective-permute-start | bytes 1572872 | tf_op jit(solution)/shard_map/ppermute | solution.py:47
  137.7 18.9 %collective-permute-start.17 = (bf16[2,512,256]{2,1,0:T(8,128)(2,1)S(1)}, bf16[2,512,256]{2,1,0:T(8,128)(2,1)S(1)}, u32[]{:S(2)}, u32[]{:S(2)}) collective-permute-start(bf16[2,512,256]{2,1,0:T(8,128)(2,1)S(1)} %copy-done.32), channel_id=1, source_target_pairs={{0,6},{1,7},{2,0},{3,1},{4,2},{5,3},{6,4},{7,5},{8,14},{9,15},{10,... | collective-permute-start | bytes 1572872 | tf_op jit(solution)/shard_map/ppermute | solution.py:47
  144.7 11.8 %collective-permute-start.18 = (bf16[2,256,256]{2,1,0:T(8,128)(2,1)}, bf16[2,256,256]{2,1,0:T(8,128)(2,1)S(1)}, u32[]{:S(2)}, u32[]{:S(2)}) collective-permute-start(bf16[2,256,256]{2,1,0:T(8,128)(2,1)} %get-tuple-element.71), channel_id=1, source_target_pairs={{0,2},{1,3},{2,4},{3,5},{4,6},{5,7},{6,0},{7,1},{8,10},{9,11},{10,... | collective-permute-start | bytes 786440 | tf_op jit(solution)/shard_map/ppermute | solution.py:47
  144.8 11.8 %collective-permute-start.19 = (bf16[2,256,256]{2,1,0:T(8,128)(2,1)}, bf16[2,256,256]{2,1,0:T(8,128)(2,1)S(1)}, u32[]{:S(2)}, u32[]{:S(2)}) collective-permute-start(bf16[2,256,256]{2,1,0:T(8,128)(2,1)} %get-tuple-element.73), channel_id=1, source_target_pairs={{0,6},{1,7},{2,0},{3,1},{4,2},{5,3},{6,4},{7,5},{8,14},{9,15},{10,... | collective-permute-start | bytes 786440 | tf_op jit(solution)/shard_map/ppermute | solution.py:47
  163.1 19.1 %collective-permute-start.21 = (bf16[2,512,256]{2,1,0:T(8,128)(2,1)}, bf16[2,512,256]{2,1,0:T(8,128)(2,1)S(1)}, u32[]{:S(2)}, u32[]{:S(2)}) collective-permute-start(bf16[2,512,256]{2,1,0:T(8,128)(2,1)} %get-tuple-element.75), channel_id=1, source_target_pairs={{0,2},{1,3},{2,4},{3,5},{4,6},{5,7},{6,0},{7,1},{8,10},{9,11},{10,... | collective-permute-start | bytes 1572872 | tf_op jit(solution)/shard_map/ppermute | solution.py:47
  163.4 18.9 %collective-permute-start.22 = (bf16[2,512,256]{2,1,0:T(8,128)(2,1)}, bf16[2,512,256]{2,1,0:T(8,128)(2,1)S(1)}, u32[]{:S(2)}, u32[]{:S(2)}) collective-permute-start(bf16[2,512,256]{2,1,0:T(8,128)(2,1)} %get-tuple-element.80), channel_id=1, source_target_pairs={{0,6},{1,7},{2,0},{3,1},{4,2},{5,3},{6,4},{7,5},{8,14},{9,15},{10,... | collective-permute-start | bytes 1572872 | tf_op jit(solution)/shard_map/ppermute | solution.py:47
  166.4 15.8 %collective-permute-start.20 = (bf16[1,640,256]{2,1,0:T(8,128)(2,1)S(1)}, bf16[1,640,256]{2,1,0:T(8,128)(2,1)S(1)}, u32[]{:S(2)}, u32[]{:S(2)}) collective-permute-start(bf16[1,640,256]{2,1,0:T(8,128)(2,1)S(1)} %copy-done.4), channel_id=1, source_target_pairs={{0,1},{1,0},{2,3},{3,2},{4,5},{5,4},{6,7},{7,6},{8,9},{9,8},{10,11... | collective-permute-start | bytes 983048 | tf_op jit(solution)/shard_map/ppermute | solution.py:51
  172.3 9.9 %collective-permute-start.23 = (bf16[2,256,256]{2,1,0:T(8,128)(2,1)}, bf16[2,256,256]{2,1,0:T(8,128)(2,1)S(1)}, u32[]{:S(2)}, u32[]{:S(2)}) collective-permute-start(bf16[2,256,256]{2,1,0:T(8,128)(2,1)} %get-tuple-element.77), channel_id=1, source_target_pairs={{0,2},{1,3},{2,4},{3,5},{4,6},{5,7},{6,0},{7,1},{8,10},{9,11},{10,... | collective-permute-start | bytes 786440 | tf_op jit(solution)/shard_map/ppermute | solution.py:47
  172.3 9.9 %collective-permute-start.24 = (bf16[2,256,256]{2,1,0:T(8,128)(2,1)}, bf16[2,256,256]{2,1,0:T(8,128)(2,1)S(1)}, u32[]{:S(2)}, u32[]{:S(2)}) collective-permute-start(bf16[2,256,256]{2,1,0:T(8,128)(2,1)} %get-tuple-element.81), channel_id=1, source_target_pairs={{0,6},{1,7},{2,0},{3,1},{4,2},{5,3},{6,4},{7,5},{8,14},{9,15},{10,... | collective-permute-start | bytes 786440 | tf_op jit(solution)/shard_map/ppermute | solution.py:47
  188.8 16.6 %collective-permute-start.25 = (bf16[2,512,256]{2,1,0:T(8,128)(2,1)}, bf16[2,512,256]{2,1,0:T(8,128)(2,1)S(1)}, u32[]{:S(2)}, u32[]{:S(2)}) collective-permute-start(bf16[2,512,256]{2,1,0:T(8,128)(2,1)} %get-tuple-element.83), channel_id=1, source_target_pairs={{0,2},{1,3},{2,4},{3,5},{4,6},{5,7},{6,0},{7,1},{8,10},{9,11},{10,... | collective-permute-start | bytes 1572872 | tf_op jit(solution)/shard_map/ppermute | solution.py:47
  189.1 16.4 %collective-permute-start.26 = (bf16[2,512,256]{2,1,0:T(8,128)(2,1)}, bf16[2,512,256]{2,1,0:T(8,128)(2,1)S(1)}, u32[]{:S(2)}, u32[]{:S(2)}) collective-permute-start(bf16[2,512,256]{2,1,0:T(8,128)(2,1)} %get-tuple-element.89), channel_id=1, source_target_pairs={{0,6},{1,7},{2,0},{3,1},{4,2},{5,3},{6,4},{7,5},{8,14},{9,15},{10,... | collective-permute-start | bytes 1572872 | tf_op jit(solution)/shard_map/ppermute | solution.py:47
  195.6 9.9 %collective-permute-start.27 = (bf16[1,256,256]{2,1,0:T(8,128)(2,1)}, bf16[1,256,256]{2,1,0:T(8,128)(2,1)S(1)}, u32[]{:S(2)}, u32[]{:S(2)}) collective-permute-start(bf16[1,256,256]{2,1,0:T(8,128)(2,1)} %get-tuple-element.85), channel_id=1, source_target_pairs={{0,2},{1,3},{2,4},{3,5},{4,6},{5,7},{6,0},{7,1},{8,10},{9,11},{10,... | collective-permute-start | bytes 393224 | tf_op jit(solution)/shard_map/ppermute | solution.py:47
  195.6 9.9 %collective-permute-start.28 = (bf16[1,256,256]{2,1,0:T(8,128)(2,1)}, bf16[1,256,256]{2,1,0:T(8,128)(2,1)S(1)}, u32[]{:S(2)}, u32[]{:S(2)}) collective-permute-start(bf16[1,256,256]{2,1,0:T(8,128)(2,1)} %get-tuple-element.90), channel_id=1, source_target_pairs={{0,6},{1,7},{2,0},{3,1},{4,2},{5,3},{6,4},{7,5},{8,14},{9,15},{10,... | collective-permute-start | bytes 393224 | tf_op jit(solution)/shard_map/ppermute | solution.py:47
  210.6 9.9 %collective-permute-start.29 = (bf16[1,512,256]{2,1,0:T(8,128)(2,1)}, bf16[1,512,256]{2,1,0:T(8,128)(2,1)S(1)}, u32[]{:S(2)}, u32[]{:S(2)}) collective-permute-start(bf16[1,512,256]{2,1,0:T(8,128)(2,1)} %get-tuple-element.92), channel_id=1, source_target_pairs={{0,2},{1,3},{2,4},{3,5},{4,6},{5,7},{6,0},{7,1},{8,10},{9,11},{10,... | collective-permute-start | bytes 786440 | tf_op jit(solution)/shard_map/ppermute | solution.py:47
  210.7 9.8 %collective-permute-start.30 = (bf16[1,512,256]{2,1,0:T(8,128)(2,1)}, bf16[1,512,256]{2,1,0:T(8,128)(2,1)S(1)}, u32[]{:S(2)}, u32[]{:S(2)}) collective-permute-start(bf16[1,512,256]{2,1,0:T(8,128)(2,1)} %get-tuple-element.96), channel_id=1, source_target_pairs={{0,6},{1,7},{2,0},{3,1},{4,2},{5,3},{6,4},{7,5},{8,14},{9,15},{10,... | collective-permute-start | bytes 786440 | tf_op jit(solution)/shard_map/ppermute | solution.py:47
  (35 other events, 151.3 us)
Sparse Core Ops, SparseCore 0:
  17.7 40.8 all-gather.1
  133.4 73.8 reduce-scatter.1

commit v2 on v1

--- a/solution.py
+++ b/solution.py
@@ -440,14 +440,13 @@
     steps = (1, -1, 2)
     beside = over_x_lo(left)
     line = [right, *[over_y(right, step) for step in steps]]
-    masked = mask_weights(where, weights, tile_mask, 0, 512, None)
-    masked = mask_weights(after(where, received, masked), weights, tile_mask, 512, 1536, masked)
+    masked = mask_weights(after(where, received), weights, tile_mask, 0, 768, None)
     pair = after(jnp.stack([left, beside]), masked)
     pairs = [pair, *[over_y(pair, step) for step in steps]]
     line = after(jnp.stack(line), masked)
     lines = [line, over_x_lo(line)]
     cot = cotangent.reshape(8, 2, rows, -1).transpose(1, 0, 2, 3).reshape(cotangent.shape)
-    masked = mask_weights(after(where, pair, line, cot), weights, tile_mask, 1536, width, masked)
+    masked = mask_weights(after(where, pair, line, cot), weights, tile_mask, 768, width, masked)
     order = (0, 3, 1, 2)
     here = after(where, masked)
     mine_l = place(here, pairs, [[(0, dy), (1, dy)] for dy in order])

time: 234 us -> 234 us (level)
    unnamed x70 -> x72, local copies, waits for them, and re-layouts: 10.5 us -> 9.81 us
    pallas_call x3 -> x2, Pallas kernels: 23 us -> 22.8 us  [mask_weights(): pl.pallas_call(functools.partial(mask_body, rows // TILE, units, begin),...]
  transfers between devices with their start and end apart: 33 -> 33, of which waited for: 6 -> 7; matrix products, arithmetic and copies ran while one was open for 2% -> 2% of each run, Pallas kernels for 53% -> 53%
where the time goes in v2:
time: 234 us; the launch traced here: 233 us
  Pallas kernels  129 us (55%)
  starting transfers between devices  52.7 us (23%)
  waiting for transfers between devices  21.7 us (9%)
  local copies, waits for them, and re-layouts  14.8 us (6%)
  between operations  14.5 us (6%)
    ppermute x16, starting transfers between devices, over_z(): lax.ppermute(v, 'replica', [(i, (i + 2 * step) % 8) for i in range(8)])  26.1 us
    pallas_call x4, Pallas kernels, last_rows(): pl.pallas_call(functools.partial(last_body, count, first, 1.0 / math.sqrt...  24.4 us
    pallas_call x2, Pallas kernels, mask_weights(): pl.pallas_call(functools.partial(mask_body, rows // TILE, units, begin),...  22.8 us
    pallas_call x4, Pallas kernels, near_rows(): pl.pallas_call(functools.partial(near_body, count), grid_spec=pltpu.Prefe...  21.6 us
    pallas_call x1, Pallas kernels, token_rows(): pl.pallas_call(functools.partial(token_body, len(gs)), grid_spec=pltpu.Pr...  16.1 us
    pallas_call x4, Pallas kernels, far_rows(): pl.pallas_call(functools.partial(far_body, count), grid_spec=pltpu.Prefet...  15.8 us
    pallas_call x1, Pallas kernels, rest_grads(): pl.pallas_call(functools.partial(rest_body, counts), grid_spec=pltpu.Pref...  13.1 us
    ppermute x5, waiting for transfers between devices, over_x_hi(): return lax.ppermute(v, 'replica', [(i, i ^ 1) for i in range(8)])  13 us
  transfers between devices with their start and end apart: 33, of which 7 were waited for; matrix products, arithmetic and copies ran while one was open for 2% of the time, Pallas kernels for 53%

profile of v2, /device:TPU:0, one launch (start us, length us, event | category | flops | bytes accessed | tf_op | source)
XLA Modules:
  0.0 232.6 jit_solution(4394067966973558484)
XLA Ops:
  9.5 3.2 %collective-permute-start.1 = (bf16[40,2048]{1,0:T(8,128)(2,1)S(1)}, bf16[40,2048]{1,0:T(8,128)(2,1)S(1)}, u32[]{:S(2)}, u32[]{:S(2)}) collective-permute-start(bf16[40,2048]{1,0:T(8,128)(2,1)S(1)} %bitcast.53), channel_id=1, source_target_pairs={{0,1},{1,0},{2,3},{3,2},{4,5},{5,4},{6,7},{7,6},{8,9},{9,8},{10,11... | collective-permute-start | bytes 491528 | tf_op jit(solution)/shard_map/ppermute | solution.py:51
  12.7 4.2 %collective-permute-done.1 = bf16[40,2048]{1,0:T(8,128)(2,1)S(1)} collective-permute-done((bf16[40,2048]{1,0:T(8,128)(2,1)S(1)}, bf16[40,2048]{1,0:T(8,128)(2,1)S(1)}, u32[]{:S(2)}, u32[]{:S(2)}) %collective-permute-start.1) | collective-permute-done | bytes 163872 | tf_op jit(solution)/shard_map/ppermute | solution.py:51
  18.7 3.5 %collective-permute-start.4 = (bf16[40,2048]{1,0:T(8,128)(2,1)S(1)}, bf16[40,2048]{1,0:T(8,128)(2,1)S(1)}, u32[]{:S(2)}, u32[]{:S(2)}) collective-permute-start(bf16[40,2048]{1,0:T(8,128)(2,1)S(1)} %get-tuple-element.104), channel_id=1, source_target_pairs={{0,32},{8,40},{16,48},{24,56},{32,0},{40,8},{48,16},{56,24},{64,96... | collective-permute-start | bytes 491528 | tf_op jit(solution)/shard_map/ppermute | solution.py:43
  29.6 5.8 %mask_weights.2.rest_0_ = bf16[7,4096,256]{2,1,0:T(8,128)(2,1)} custom-call(s32[5]{0:T(128)} %stack.47.where, s32[32,2,7]{2,1,0:T(2,128)} %copy.16.mask_ref, bf16[4096,2,896]{2,1,0:T(2,128)(2,1)} %w_ref.11), custom_call_target="tpu_custom_call" | custom-call | flops 1 | bytes 1 | tf_op jit(solution)/shard_map/mask_weights/pallas_call | solution.py:113
  42.7 17.1 %mask_weights.3.w_ref.refs_4_ = bf16[7,4096,256]{2,1,0:T(8,128)(2,1)} custom-call(s32[5]{0:T(128)} %stack.47.where, s32[32,2,7]{2,1,0:T(2,128)} %copy.16.mask_ref, bf16[4096,2,896]{2,1,0:T(2,128)(2,1)} %w_ref.11, bf16[7,4096,256]{2,1,0:T(8,128)(2,1)} %mask_weights.2.rest_0_), custom_call_target="tpu_custom_call", output_to_operand_aliasing={{}: (3, {})} | custom-call | flops 1 | bytes 1 | tf_op jit(solution)/shard_map/mask_weights/pallas_call | solution.py:113
  63.2 3.0 %place.2 = bf16[8,40,2048]{2,1,0:T(8,128)(2,1)} custom-call(s32[5]{0:T(128)} %stack.47.where, bf16[2,40,2048]{2,1,0:T(8,128)(2,1)} %copy-done.9, bf16[2,40,2048]{2,1,0:T(8,128)(2,1)} %copy-done.18, bf16[2,40,2048]{2,1,0:T(8,128)(2,1)} %copy-done.19, bf16[2,40,2048]{2,1,0:T(8,128)(2,1)} %copy-done.20), custom_call_target="tpu_custom_call" | custom-call | flops 1 | bytes 1 | tf_op jit(solution)/shard_map/place/pallas_call | solution.py:80
  67.0 2.9 %place.3 = bf16[8,40,2048]{2,1,0:T(8,128)(2,1)} custom-call(s32[5]{0:T(128)} %stack.47.where, bf16[4,40,2048]{2,1,0:T(8,128)(2,1)} %copy-done.6, bf16[4,40,2048]{2,1,0:T(8,128)(2,1)} %copy-done.11), custom_call_target="tpu_custom_call" | custom-call | flops 1 | bytes 1 | tf_op jit(solution)/shard_map/place/pallas_call | solution.py:80
  70.5 2.9 %collective-permute-done.10.theirs_r = bf16[320,2048]{1,0:T(8,128)(2,1)S(1)} collective-permute-done((bf16[320,2048]{1,0:T(8,128)(2,1)}, bf16[320,2048]{1,0:T(8,128)(2,1)S(1)}, u32[]{:S(2)}, u32[]{:S(2)}) %collective-permute-start.10) | collective-permute-done | bytes 1310752 | tf_op jit(solution)/shard_map/ppermute | solution.py:34
  74.4 9.1 %first_grads.1 = (bf16[2,640,256]{2,1,0:T(8,128)(2,1)}, bf16[2,320,4096]{2,1,0:T(8,128)(2,1)}) custom-call(s32[5]{0:T(128)} %stack.47.where, bf16[320,2048]{1,0:T(8,128)(2,1)} %bitcast.44, bf16[320,2048]{1,0:T(8,128)(2,1)} %copy-done.7, bf16[320,2048]{1,0:T(8,128)(2,1)} %bitcast.46, bf16[320,2048]{1,0:T(8,128)(2,1)} %copy-done.8, ...), custom_call_target="tpu_custom_call" | custom-call | flops 1 | bytes 1 | tf_op jit(solution)/shard_map/first_grads/pallas_call | solution.py:175
  83.5 2.8 %collective-permute-start.11 = (bf16[2,640,256]{2,1,0:T(8,128)(2,1)}, bf16[2,640,256]{2,1,0:T(8,128)(2,1)S(1)}, u32[]{:S(2)}, u32[]{:S(2)}) collective-permute-start(bf16[2,640,256]{2,1,0:T(8,128)(2,1)} %get-tuple-element.60.g_a.refs_0_), channel_id=1, source_target_pairs={{0,1},{1,0},{2,3},{3,2},{4,5},{5,4},{6,7},{7,6},{8,9},{9,8},{10,11... | collective-permute-start | bytes 1966088 | tf_op jit(solution)/shard_map/ppermute | solution.py:51
  86.2 13.1 %rest_grads.1 = (bf16[2,640,256]{2,1,0:T(8,128)(2,1)}, bf16[2,640,256]{2,1,0:T(8,128)(2,1)}, bf16[1,640,256]{2,1,0:T(8,128)(2,1)}) custom-call(s32[5]{0:T(128)} %stack.47.where, bf16[640,4096]{1,0:T(8,128)(2,1)} %bitcast.23, bf16[7,4096,256]{2,1,0:T(8,128)(2,1)} %mask_weights.3.w_ref.refs_4_, bf16[640,896]{1,0:T(8,128)(2,1)} %bitcast.42), custom_call_target="tpu_custom_call" | custom-call | flops 1 | bytes 1 | tf_op jit(solution)/shard_map/rest_grads/pallas_call | solution.py:228
  103.1 4.1 %far_rows.4 = (bf16[2,256,256]{2,1,0:T(8,128)(2,1)}, bf16[2,256,256]{2,1,0:T(8,128)(2,1)}) custom-call(s32[5]{0:T(128)} %stack.47.where, bf16[640,4096]{1,0:T(8,128)(2,1)} %bitcast.24, bf16[640,2048]{1,0:T(8,128)(2,1)} %all-gather.2.cloned.1.call-done.tok_b.tok_ub.tok_db, bf16[2,640,256]{2,1,0:T(8,128)(2,1)} %get-tuple-element.60.g_a.refs_0_, ...), custom_call_target="tpu_custom_call" | custom-call | flops 1 | bytes 1 | tf_op jit(solution)/shard_map/far_rows/pallas_call | solution.py:309
  110.4 16.1 %token_rows.1 = bf16[16,40,4096]{2,1,0:T(8,128)(2,1)} custom-call(s32[5]{0:T(128)} %stack.47.where, bf16[2,640,256]{2,1,0:T(8,128)(2,1)} %get-tuple-element.60.g_a.refs_0_, bf16[2,640,256]{2,1,0:T(8,128)(2,1)} %get-tuple-element.59.refs_1_.g_a, bf16[2,640,256]{2,1,0:T(8,128)(2,1)} %get-tuple-element.64.refs_2_.g_a, ...), custom_call_target="tpu_custom_call" | custom-call | flops 1 | bytes 1 | tf_op jit(solution)/shard_map/token_rows/pallas_call | solution.py:412
  127.4 5.7 %near_rows.4 = (bf16[2,512,256]{2,1,0:T(8,128)(2,1)}, bf16[2,512,256]{2,1,0:T(8,128)(2,1)}) custom-call(s32[5]{0:T(128)} %stack.47.where, bf16[640,4096]{1,0:T(8,128)(2,1)} %bitcast.25, bf16[640,2048]{1,0:T(8,128)(2,1)} %all-gather.2.cloned.1.call-done.tok_b.tok_ub.tok_db, bf16[640,4096]{1,0:T(8,128)(2,1)} %bitcast.26, ...), custom_call_target="tpu_custom_call" | custom-call | flops 1 | bytes 1 | tf_op jit(solution)/shard_map/near_rows/pallas_call | solution.py:327
  134.2 3.0 %collective-permute-start.15 = (bf16[2,640,256]{2,1,0:T(8,128)(2,1)S(1)}, bf16[2,640,256]{2,1,0:T(8,128)(2,1)S(1)}, u32[]{:S(2)}, u32[]{:S(2)}) collective-permute-start(bf16[2,640,256]{2,1,0:T(8,128)(2,1)S(1)} %copy-done), channel_id=1, source_target_pairs={{0,1},{1,0},{2,3},{3,2},{4,5},{5,4},{6,7},{7,6},{8,9},{9,8},{10,11... | collective-permute-start | bytes 1966088 | tf_op jit(solution)/shard_map/ppermute | solution.py:51
  140.5 4.1 %far_rows.5 = (bf16[2,256,256]{2,1,0:T(8,128)(2,1)}, bf16[2,256,256]{2,1,0:T(8,128)(2,1)}) custom-call(s32[5]{0:T(128)} %stack.47.where, bf16[640,4096]{1,0:T(8,128)(2,1)} %bitcast.27, bf16[640,2048]{1,0:T(8,128)(2,1)} %all-gather.2.cloned.1.call-done.tok_b.tok_ub.tok_db, bf16[2,640,256]{2,1,0:T(8,128)(2,1)} %get-tuple-element.59.refs_1_.g_a, ...), custom_call_target="tpu_custom_call" | custom-call | flops 1 | bytes 1 | tf_op jit(solution)/shard_map/far_rows/pallas_call | solution.py:309
  144.6 3.2 %collective-permute-start.19 = (bf16[2,256,256]{2,1,0:T(8,128)(2,1)}, bf16[2,256,256]{2,1,0:T(8,128)(2,1)S(1)}, u32[]{:S(2)}, u32[]{:S(2)}) collective-permute-start(bf16[2,256,256]{2,1,0:T(8,128)(2,1)} %get-tuple-element.73), channel_id=1, source_target_pairs={{0,6},{1,7},{2,0},{3,1},{4,2},{5,3},{6,4},{7,5},{8,14},{9,15},{10,... | collective-permute-start | bytes 786440 | tf_op jit(solution)/shard_map/ppermute | solution.py:47
  147.8 6.7 %collective-permute-done.15.g_b = bf16[2,640,256]{2,1,0:T(8,128)(2,1)S(1)} collective-permute-done((bf16[2,640,256]{2,1,0:T(8,128)(2,1)S(1)}, bf16[2,640,256]{2,1,0:T(8,128)(2,1)S(1)}, u32[]{:S(2)}, u32[]{:S(2)}) %collective-permute-start.15) | collective-permute-done | bytes 655392 | tf_op jit(solution)/shard_map/ppermute | solution.py:51
  157.2 5.7 %near_rows.5 = (bf16[2,512,256]{2,1,0:T(8,128)(2,1)}, bf16[2,512,256]{2,1,0:T(8,128)(2,1)}) custom-call(s32[5]{0:T(128)} %stack.47.where, bf16[640,4096]{1,0:T(8,128)(2,1)} %bitcast.28, bf16[640,2048]{1,0:T(8,128)(2,1)} %all-gather.2.cloned.1.call-done.tok_b.tok_ub.tok_db, bf16[640,4096]{1,0:T(8,128)(2,1)} %bitcast.29, ...), custom_call_target="tpu_custom_call" | custom-call | flops 1 | bytes 1 | tf_op jit(solution)/shard_map/near_rows/pallas_call | solution.py:327
  163.3 2.9 %collective-permute-start.22 = (bf16[2,512,256]{2,1,0:T(8,128)(2,1)}, bf16[2,512,256]{2,1,0:T(8,128)(2,1)S(1)}, u32[]{:S(2)}, u32[]{:S(2)}) collective-permute-start(bf16[2,512,256]{2,1,0:T(8,128)(2,1)} %get-tuple-element.80), channel_id=1, source_target_pairs={{0,6},{1,7},{2,0},{3,1},{4,2},{5,3},{6,4},{7,5},{8,14},{9,15},{10,... | collective-permute-start | bytes 1572872 | tf_op jit(solution)/shard_map/ppermute | solution.py:47
  168.0 4.1 %far_rows.6 = (bf16[2,256,256]{2,1,0:T(8,128)(2,1)}, bf16[2,256,256]{2,1,0:T(8,128)(2,1)}) custom-call(s32[5]{0:T(128)} %stack.47.where, bf16[640,4096]{1,0:T(8,128)(2,1)} %bitcast.30, bf16[640,2048]{1,0:T(8,128)(2,1)} %all-gather.2.cloned.1.call-done.tok_b.tok_ub.tok_db, bf16[2,640,256]{2,1,0:T(8,128)(2,1)} %get-tuple-element.64.refs_2_.g_a, ...), custom_call_target="tpu_custom_call" | custom-call | flops 1 | bytes 1 | tf_op jit(solution)/shard_map/far_rows/pallas_call | solution.py:309
  172.2 3.2 %collective-permute-start.24 = (bf16[2,256,256]{2,1,0:T(8,128)(2,1)}, bf16[2,256,256]{2,1,0:T(8,128)(2,1)S(1)}, u32[]{:S(2)}, u32[]{:S(2)}) collective-permute-start(bf16[2,256,256]{2,1,0:T(8,128)(2,1)} %get-tuple-element.81), channel_id=1, source_target_pairs={{0,6},{1,7},{2,0},{3,1},{4,2},{5,3},{6,4},{7,5},{8,14},{9,15},{10,... | collective-permute-start | bytes 786440 | tf_op jit(solution)/shard_map/ppermute | solution.py:47
  175.4 6.6 %last_rows.4 = (bf16[512,2,896]{2,1,0:T(2,128)(2,1)}, f32[512,2,896]{2,1,0:T(2,128)}) custom-call(s32[5]{0:T(128)} %stack.47.where, s32[32,2,7]{2,1,0:T(2,128)} %copy.16.mask_ref, bf16[640,4096]{1,0:T(8,128)(2,1)} %bitcast.31, bf16[640,2048]{1,0:T(8,128)(2,1)} %all-gather.2.cloned.1.call-done.tok_b.tok_ub.tok_db, ...), custom_call_target="tpu_custom_call" | custom-call | flops 1 | bytes 1 | tf_op jit(solution)/shard_map/last_rows/pallas_call | solution.py:373
  182.9 5.7 %near_rows.6 = (bf16[2,512,256]{2,1,0:T(8,128)(2,1)}, bf16[2,512,256]{2,1,0:T(8,128)(2,1)}) custom-call(s32[5]{0:T(128)} %stack.47.where, bf16[640,4096]{1,0:T(8,128)(2,1)} %bitcast.32, bf16[640,2048]{1,0:T(8,128)(2,1)} %all-gather.2.cloned.1.call-done.tok_b.tok_ub.tok_db, bf16[640,4096]{1,0:T(8,128)(2,1)} %bitcast.33, ...), custom_call_target="tpu_custom_call" | custom-call | flops 1 | bytes 1 | tf_op jit(solution)/shard_map/near_rows/pallas_call | solution.py:327
  188.8 3.1 %collective-permute-start.26 = (bf16[2,512,256]{2,1,0:T(8,128)(2,1)}, bf16[2,512,256]{2,1,0:T(8,128)(2,1)S(1)}, u32[]{:S(2)}, u32[]{:S(2)}) collective-permute-start(bf16[2,512,256]{2,1,0:T(8,128)(2,1)} %get-tuple-element.89), channel_id=1, source_target_pairs={{0,6},{1,7},{2,0},{3,1},{4,2},{5,3},{6,4},{7,5},{8,14},{9,15},{10,... | collective-permute-start | bytes 1572872 | tf_op jit(solution)/shard_map/ppermute | solution.py:47
  191.9 3.5 %far_rows.7 = (bf16[1,256,256]{2,1,0:T(8,128)(2,1)}, bf16[1,256,256]{2,1,0:T(8,128)(2,1)}) custom-call(s32[5]{0:T(128)} %stack.47.where, bf16[640,4096]{1,0:T(8,128)(2,1)} %bitcast.34, bf16[640,2048]{1,0:T(8,128)(2,1)} %all-gather.2.cloned.1.call-done.tok_b.tok_ub.tok_db, bf16[1,640,256]{2,1,0:T(8,128)(2,1)} %get-tuple-element.65.refs_3_.g_a, ...), custom_call_target="tpu_custom_call" | custom-call | flops 1 | bytes 1 | tf_op jit(solution)/shard_map/far_rows/pallas_call | solution.py:309
  195.4 3.2 %collective-permute-start.28 = (bf16[1,256,256]{2,1,0:T(8,128)(2,1)}, bf16[1,256,256]{2,1,0:T(8,128)(2,1)S(1)}, u32[]{:S(2)}, u32[]{:S(2)}) collective-permute-start(bf16[1,256,256]{2,1,0:T(8,128)(2,1)} %get-tuple-element.90), channel_id=1, source_target_pairs={{0,6},{1,7},{2,0},{3,1},{4,2},{5,3},{6,4},{7,5},{8,14},{9,15},{10,... | collective-permute-start | bytes 393224 | tf_op jit(solution)/shard_map/ppermute | solution.py:47
  198.6 6.6 %last_rows.5 = (bf16[512,2,896]{2,1,0:T(2,128)(2,1)}, f32[512,2,896]{2,1,0:T(2,128)}) custom-call(s32[5]{0:T(128)} %stack.47.where, s32[32,2,7]{2,1,0:T(2,128)} %copy.16.mask_ref, bf16[640,4096]{1,0:T(8,128)(2,1)} %bitcast.35, bf16[640,2048]{1,0:T(8,128)(2,1)} %all-gather.2.cloned.1.call-done.tok_b.tok_ub.tok_db, ...), custom_call_target="tpu_custom_call", output_to_operand_aliasing={{0}: (10, {}), {1}: (11, {})} | custom-call | flops 1 | bytes 1 | tf_op jit(solution)/shard_map/last_rows/pallas_call | solution.py:373
  205.9 4.5 %near_rows.7 = (bf16[1,512,256]{2,1,0:T(8,128)(2,1)}, bf16[1,512,256]{2,1,0:T(8,128)(2,1)}) custom-call(s32[5]{0:T(128)} %stack.47.where, bf16[640,4096]{1,0:T(8,128)(2,1)} %bitcast.36, bf16[640,2048]{1,0:T(8,128)(2,1)} %all-gather.2.cloned.1.call-done.tok_b.tok_ub.tok_db, bf16[640,4096]{1,0:T(8,128)(2,1)} %bitcast.37, ...), custom_call_target="tpu_custom_call" | custom-call | flops 1 | bytes 1 | tf_op jit(solution)/shard_map/near_rows/pallas_call | solution.py:327
  210.5 3.2 %collective-permute-start.30 = (bf16[1,512,256]{2,1,0:T(8,128)(2,1)}, bf16[1,512,256]{2,1,0:T(8,128)(2,1)S(1)}, u32[]{:S(2)}, u32[]{:S(2)}) collective-permute-start(bf16[1,512,256]{2,1,0:T(8,128)(2,1)} %get-tuple-element.96), channel_id=1, source_target_pairs={{0,6},{1,7},{2,0},{3,1},{4,2},{5,3},{6,4},{7,5},{8,14},{9,15},{10,... | collective-permute-start | bytes 786440 | tf_op jit(solution)/shard_map/ppermute | solution.py:47
  213.7 6.6 %last_rows.6 = (bf16[512,2,896]{2,1,0:T(2,128)(2,1)}, f32[512,2,896]{2,1,0:T(2,128)}) custom-call(s32[5]{0:T(128)} %stack.47.where, s32[32,2,7]{2,1,0:T(2,128)} %copy.16.mask_ref, bf16[640,4096]{1,0:T(8,128)(2,1)} %bitcast.38, bf16[640,2048]{1,0:T(8,128)(2,1)} %all-gather.2.cloned.1.call-done.tok_b.tok_ub.tok_db, ...), custom_call_target="tpu_custom_call", output_to_operand_aliasing={{0}: (10, {}), {1}: (11, {})} | custom-call | flops 1 | bytes 1 | tf_op jit(solution)/shard_map/last_rows/pallas_call | solution.py:373
  221.1 4.6 %last_rows.7 = (bf16[512,2,896]{2,1,0:T(2,128)(2,1)}, f32[512,2,896]{2,1,0:T(2,128)}) custom-call(s32[5]{0:T(128)} %stack.47.where, s32[32,2,7]{2,1,0:T(2,128)} %copy.16.mask_ref, bf16[640,4096]{1,0:T(8,128)(2,1)} %bitcast.39, bf16[640,2048]{1,0:T(8,128)(2,1)} %all-gather.2.cloned.1.call-done.tok_b.tok_ub.tok_db, ...), custom_call_target="tpu_custom_call", output_to_operand_aliasing={{0}: (10, {}), {1}: (11, {})} | custom-call | flops 1 | bytes 1 | tf_op jit(solution)/shard_map/last_rows/pallas_call | solution.py:373
  (134 shorter events, 44.1 us)
Async XLA Ops:
  7.2 95.1 %all-gather.2.cloned.1.call-start = ((), (), s32[]{:S(2)}) async-start(), calls=%async_computation.1 | async-start | bytes 2785280 | tf_op jit(solution)/shard_map/all_gather | solution.py:437
  9.5 7.4 %collective-permute-start.1 = (bf16[40,2048]{1,0:T(8,128)(2,1)S(1)}, bf16[40,2048]{1,0:T(8,128)(2,1)S(1)}, u32[]{:S(2)}, u32[]{:S(2)}) collective-permute-start(bf16[40,2048]{1,0:T(8,128)(2,1)S(1)} %bitcast.53), channel_id=1, source_target_pairs={{0,1},{1,0},{2,3},{3,2},{4,5},{5,4},{6,7},{7,6},{8,9},{9,8},{10,11... | collective-permute-start | bytes 491528 | tf_op jit(solution)/shard_map/ppermute | solution.py:51
  17.6 208.1 %reduce-scatter.2.cloned.1.call-start = ((), (), s32[]{:S(2)}) async-start(), calls=%async_computation.2 | async-start | bytes 5570560 | tf_op jit(solution)/shard_map/reduce_scatter | solution.py:479
  18.7 9.5 %collective-permute-start.4 = (bf16[40,2048]{1,0:T(8,128)(2,1)S(1)}, bf16[40,2048]{1,0:T(8,128)(2,1)S(1)}, u32[]{:S(2)}, u32[]{:S(2)}) collective-permute-start(bf16[40,2048]{1,0:T(8,128)(2,1)S(1)} %get-tuple-element.104), channel_id=1, source_target_pairs={{0,32},{8,40},{16,48},{24,56},{32,0},{40,8},{48,16},{56,24},{64,96... | collective-permute-start | bytes 491528 | tf_op jit(solution)/shard_map/ppermute | solution.py:43
  22.2 7.3 %collective-permute-start.2 = (bf16[40,2048]{1,0:T(8,128)(2,1)S(1)}, bf16[40,2048]{1,0:T(8,128)(2,1)S(1)}, u32[]{:S(2)}, u32[]{:S(2)}) collective-permute-start(bf16[40,2048]{1,0:T(8,128)(2,1)S(1)} %get-tuple-element.104), channel_id=1, source_target_pairs={{0,16},{8,24},{16,32},{24,40},{32,48},{40,56},{48,0},{56,8},{64,80... | collective-permute-start | bytes 491528 | tf_op jit(solution)/shard_map/ppermute | solution.py:43
  22.9 6.6 %collective-permute-start.3 = (bf16[40,2048]{1,0:T(8,128)(2,1)S(1)}, bf16[40,2048]{1,0:T(8,128)(2,1)S(1)}, u32[]{:S(2)}, u32[]{:S(2)}) collective-permute-start(bf16[40,2048]{1,0:T(8,128)(2,1)S(1)} %get-tuple-element.104), channel_id=1, source_target_pairs={{0,48},{8,56},{16,0},{24,8},{32,16},{40,24},{48,32},{56,40},{64,11... | collective-permute-start | bytes 491528 | tf_op jit(solution)/shard_map/ppermute | solution.py:43
  25.5 11.6 %collective-permute-start = (bf16[40,2048]{1,0:T(8,128)(2,1)S(1)}, bf16[40,2048]{1,0:T(8,128)(2,1)S(1)}, u32[]{:S(2)}, u32[]{:S(2)}) collective-permute-start(bf16[40,2048]{1,0:T(8,128)(2,1)S(1)} %get-tuple-element.103), channel_id=1, source_target_pairs={{0,64},{8,72},{16,80},{24,88},{32,96},{40,104},{48,112},{56,120},{... | collective-permute-start | bytes 491528 | tf_op jit(solution)/shard_map/ppermute | solution.py:38
  35.4 30.8 %collective-permute-start.9 = (bf16[4,40,2048]{2,1,0:T(8,128)(2,1)S(1)}, bf16[4,40,2048]{2,1,0:T(8,128)(2,1)S(1)}, u32[]{:S(2)}, u32[]{:S(2)}) collective-permute-start(bf16[4,40,2048]{2,1,0:T(8,128)(2,1)S(1)} %pad_maximum_fusion.refs_0_), channel_id=1, source_target_pairs={{0,64},{8,72},{16,80},{24,88},{32,96},{40,104},{48,112},{56,120},{... | collective-permute-start | bytes 1966088 | tf_op jit(solution)/shard_map/ppermute | solution.py:38
  37.1 22.7 %collective-permute-start.5 = (bf16[2,40,2048]{2,1,0:T(8,128)(2,1)S(1)}, bf16[2,40,2048]{2,1,0:T(8,128)(2,1)S(1)}, u32[]{:S(2)}, u32[]{:S(2)}) collective-permute-start(bf16[2,40,2048]{2,1,0:T(8,128)(2,1)S(1)} %pad_maximum_fusion.1.refs_0_), channel_id=1, source_target_pairs={{0,16},{8,24},{16,32},{24,40},{32,48},{40,56},{48,0},{56,8},{64,80... | collective-permute-start | bytes 983048 | tf_op jit(solution)/shard_map/ppermute | solution.py:43
  38.4 21.5 %collective-permute-start.6 = (bf16[2,40,2048]{2,1,0:T(8,128)(2,1)S(1)}, bf16[2,40,2048]{2,1,0:T(8,128)(2,1)S(1)}, u32[]{:S(2)}, u32[]{:S(2)}) collective-permute-start(bf16[2,40,2048]{2,1,0:T(8,128)(2,1)S(1)} %pad_maximum_fusion.1.refs_0_), channel_id=1, source_target_pairs={{0,48},{8,56},{16,0},{24,8},{32,16},{40,24},{48,32},{56,40},{64,11... | collective-permute-start | bytes 983048 | tf_op jit(solution)/shard_map/ppermute | solution.py:43
  40.4 22.1 %collective-permute-start.7 = (bf16[2,40,2048]{2,1,0:T(8,128)(2,1)S(1)}, bf16[2,40,2048]{2,1,0:T(8,128)(2,1)S(1)}, u32[]{:S(2)}, u32[]{:S(2)}) collective-permute-start(bf16[2,40,2048]{2,1,0:T(8,128)(2,1)S(1)} %pad_maximum_fusion.1.refs_0_), channel_id=1, source_target_pairs={{0,32},{8,40},{16,48},{24,56},{32,0},{40,8},{48,16},{56,24},{64,96... | collective-permute-start | bytes 983048 | tf_op jit(solution)/shard_map/ppermute | solution.py:43
  66.2 4.3 %collective-permute-start.8 = (bf16[320,2048]{1,0:T(8,128)(2,1)}, bf16[320,2048]{1,0:T(8,128)(2,1)S(1)}, u32[]{:S(2)}, u32[]{:S(2)}) collective-permute-start(bf16[320,2048]{1,0:T(8,128)(2,1)} %bitcast.43), channel_id=1, source_target_pairs={{0,8},{8,0},{16,24},{24,16},{32,40},{40,32},{48,56},{56,48},{64,72... | collective-permute-start | bytes 3932168 | tf_op jit(solution)/shard_map/ppermute | solution.py:34
  83.5 18.8 %collective-permute-start.11 = (bf16[2,640,256]{2,1,0:T(8,128)(2,1)}, bf16[2,640,256]{2,1,0:T(8,128)(2,1)S(1)}, u32[]{:S(2)}, u32[]{:S(2)}) collective-permute-start(bf16[2,640,256]{2,1,0:T(8,128)(2,1)} %get-tuple-element.60.g_a.refs_0_), channel_id=1, source_target_pairs={{0,1},{1,0},{2,3},{3,2},{4,5},{5,4},{6,7},{7,6},{8,9},{9,8},{10,11... | collective-permute-start | bytes 1966088 | tf_op jit(solution)/shard_map/ppermute | solution.py:51
  99.3 27.2 %collective-permute-start.12 = (bf16[2,640,256]{2,1,0:T(8,128)(2,1)}, bf16[2,640,256]{2,1,0:T(8,128)(2,1)S(1)}, u32[]{:S(2)}, u32[]{:S(2)}) collective-permute-start(bf16[2,640,256]{2,1,0:T(8,128)(2,1)} %get-tuple-element.59.refs_1_.g_a), channel_id=1, source_target_pairs={{0,1},{1,0},{2,3},{3,2},{4,5},{5,4},{6,7},{7,6},{8,9},{9,8},{10,11... | collective-permute-start | bytes 1966088 | tf_op jit(solution)/shard_map/ppermute | solution.py:51
  107.2 19.3 %collective-permute-start.13 = (bf16[2,256,256]{2,1,0:T(8,128)(2,1)}, bf16[2,256,256]{2,1,0:T(8,128)(2,1)S(1)}, u32[]{:S(2)}, u32[]{:S(2)}) collective-permute-start(bf16[2,256,256]{2,1,0:T(8,128)(2,1)} %get-tuple-element.62), channel_id=1, source_target_pairs={{0,2},{1,3},{2,4},{3,5},{4,6},{5,7},{6,0},{7,1},{8,10},{9,11},{10,... | collective-permute-start | bytes 786440 | tf_op jit(solution)/shard_map/ppermute | solution.py:47
  108.8 17.7 %collective-permute-start.14 = (bf16[2,256,256]{2,1,0:T(8,128)(2,1)}, bf16[2,256,256]{2,1,0:T(8,128)(2,1)S(1)}, u32[]{:S(2)}, u32[]{:S(2)}) collective-permute-start(bf16[2,256,256]{2,1,0:T(8,128)(2,1)} %get-tuple-element.66), channel_id=1, source_target_pairs={{0,6},{1,7},{2,0},{3,1},{4,2},{5,3},{6,4},{7,5},{8,14},{9,15},{10,... | collective-permute-start | bytes 786440 | tf_op jit(solution)/shard_map/ppermute | solution.py:47
  134.2 20.3 %collective-permute-start.15 = (bf16[2,640,256]{2,1,0:T(8,128)(2,1)S(1)}, bf16[2,640,256]{2,1,0:T(8,128)(2,1)S(1)}, u32[]{:S(2)}, u32[]{:S(2)}) collective-permute-start(bf16[2,640,256]{2,1,0:T(8,128)(2,1)S(1)} %copy-done), channel_id=1, source_target_pairs={{0,1},{1,0},{2,3},{3,2},{4,5},{5,4},{6,7},{7,6},{8,9},{9,8},{10,11... | collective-permute-start | bytes 1966088 | tf_op jit(solution)/shard_map/ppermute | solution.py:51
  137.2 19.2 %collective-permute-start.16 = (bf16[2,512,256]{2,1,0:T(8,128)(2,1)S(1)}, bf16[2,512,256]{2,1,0:T(8,128)(2,1)S(1)}, u32[]{:S(2)}, u32[]{:S(2)}) collective-permute-start(bf16[2,512,256]{2,1,0:T(8,128)(2,1)S(1)} %copy-done.34), channel_id=1, source_target_pairs={{0,2},{1,3},{2,4},{3,5},{4,6},{5,7},{6,0},{7,1},{8,10},{9,11},{10,... | collective-permute-start | bytes 1572872 | tf_op jit(solution)/shard_map/ppermute | solution.py:47
  137.7 18.7 %collective-permute-start.17 = (bf16[2,512,256]{2,1,0:T(8,128)(2,1)S(1)}, bf16[2,512,256]{2,1,0:T(8,128)(2,1)S(1)}, u32[]{:S(2)}, u32[]{:S(2)}) collective-permute-start(bf16[2,512,256]{2,1,0:T(8,128)(2,1)S(1)} %copy-done.33), channel_id=1, source_target_pairs={{0,6},{1,7},{2,0},{3,1},{4,2},{5,3},{6,4},{7,5},{8,14},{9,15},{10,... | collective-permute-start | bytes 1572872 | tf_op jit(solution)/shard_map/ppermute | solution.py:47
  144.6 11.8 %collective-permute-start.18 = (bf16[2,256,256]{2,1,0:T(8,128)(2,1)}, bf16[2,256,256]{2,1,0:T(8,128)(2,1)S(1)}, u32[]{:S(2)}, u32[]{:S(2)}) collective-permute-start(bf16[2,256,256]{2,1,0:T(8,128)(2,1)} %get-tuple-element.71), channel_id=1, source_target_pairs={{0,2},{1,3},{2,4},{3,5},{4,6},{5,7},{6,0},{7,1},{8,10},{9,11},{10,... | collective-permute-start | bytes 786440 | tf_op jit(solution)/shard_map/ppermute | solution.py:47
  144.6 11.8 %collective-permute-start.19 = (bf16[2,256,256]{2,1,0:T(8,128)(2,1)}, bf16[2,256,256]{2,1,0:T(8,128)(2,1)S(1)}, u32[]{:S(2)}, u32[]{:S(2)}) collective-permute-start(bf16[2,256,256]{2,1,0:T(8,128)(2,1)} %get-tuple-element.73), channel_id=1, source_target_pairs={{0,6},{1,7},{2,0},{3,1},{4,2},{5,3},{6,4},{7,5},{8,14},{9,15},{10,... | collective-permute-start | bytes 786440 | tf_op jit(solution)/shard_map/ppermute | solution.py:47
  162.9 19.1 %collective-permute-start.21 = (bf16[2,512,256]{2,1,0:T(8,128)(2,1)}, bf16[2,512,256]{2,1,0:T(8,128)(2,1)S(1)}, u32[]{:S(2)}, u32[]{:S(2)}) collective-permute-start(bf16[2,512,256]{2,1,0:T(8,128)(2,1)} %get-tuple-element.75), channel_id=1, source_target_pairs={{0,2},{1,3},{2,4},{3,5},{4,6},{5,7},{6,0},{7,1},{8,10},{9,11},{10,... | collective-permute-start | bytes 1572872 | tf_op jit(solution)/shard_map/ppermute | solution.py:47
  163.3 18.8 %collective-permute-start.22 = (bf16[2,512,256]{2,1,0:T(8,128)(2,1)}, bf16[2,512,256]{2,1,0:T(8,128)(2,1)S(1)}, u32[]{:S(2)}, u32[]{:S(2)}) collective-permute-start(bf16[2,512,256]{2,1,0:T(8,128)(2,1)} %get-tuple-element.80), channel_id=1, source_target_pairs={{0,6},{1,7},{2,0},{3,1},{4,2},{5,3},{6,4},{7,5},{8,14},{9,15},{10,... | collective-permute-start | bytes 1572872 | tf_op jit(solution)/shard_map/ppermute | solution.py:47
  166.2 15.8 %collective-permute-start.20 = (bf16[1,640,256]{2,1,0:T(8,128)(2,1)S(1)}, bf16[1,640,256]{2,1,0:T(8,128)(2,1)S(1)}, u32[]{:S(2)}, u32[]{:S(2)}) collective-permute-start(bf16[1,640,256]{2,1,0:T(8,128)(2,1)S(1)} %copy-done.4), channel_id=1, source_target_pairs={{0,1},{1,0},{2,3},{3,2},{4,5},{5,4},{6,7},{7,6},{8,9},{9,8},{10,11... | collective-permute-start | bytes 983048 | tf_op jit(solution)/shard_map/ppermute | solution.py:51
  172.2 9.9 %collective-permute-start.23 = (bf16[2,256,256]{2,1,0:T(8,128)(2,1)}, bf16[2,256,256]{2,1,0:T(8,128)(2,1)S(1)}, u32[]{:S(2)}, u32[]{:S(2)}) collective-permute-start(bf16[2,256,256]{2,1,0:T(8,128)(2,1)} %get-tuple-element.77), channel_id=1, source_target_pairs={{0,2},{1,3},{2,4},{3,5},{4,6},{5,7},{6,0},{7,1},{8,10},{9,11},{10,... | collective-permute-start | bytes 786440 | tf_op jit(solution)/shard_map/ppermute | solution.py:47
  172.2 9.9 %collective-permute-start.24 = (bf16[2,256,256]{2,1,0:T(8,128)(2,1)}, bf16[2,256,256]{2,1,0:T(8,128)(2,1)S(1)}, u32[]{:S(2)}, u32[]{:S(2)}) collective-permute-start(bf16[2,256,256]{2,1,0:T(8,128)(2,1)} %get-tuple-element.81), channel_id=1, source_target_pairs={{0,6},{1,7},{2,0},{3,1},{4,2},{5,3},{6,4},{7,5},{8,14},{9,15},{10,... | collective-permute-start | bytes 786440 | tf_op jit(solution)/shard_map/ppermute | solution.py:47
  188.6 16.6 %collective-permute-start.25 = (bf16[2,512,256]{2,1,0:T(8,128)(2,1)}, bf16[2,512,256]{2,1,0:T(8,128)(2,1)S(1)}, u32[]{:S(2)}, u32[]{:S(2)}) collective-permute-start(bf16[2,512,256]{2,1,0:T(8,128)(2,1)} %get-tuple-element.83), channel_id=1, source_target_pairs={{0,2},{1,3},{2,4},{3,5},{4,6},{5,7},{6,0},{7,1},{8,10},{9,11},{10,... | collective-permute-start | bytes 1572872 | tf_op jit(solution)/shard_map/ppermute | solution.py:47
  188.8 16.4 %collective-permute-start.26 = (bf16[2,512,256]{2,1,0:T(8,128)(2,1)}, bf16[2,512,256]{2,1,0:T(8,128)(2,1)S(1)}, u32[]{:S(2)}, u32[]{:S(2)}) collective-permute-start(bf16[2,512,256]{2,1,0:T(8,128)(2,1)} %get-tuple-element.89), channel_id=1, source_target_pairs={{0,6},{1,7},{2,0},{3,1},{4,2},{5,3},{6,4},{7,5},{8,14},{9,15},{10,... | collective-permute-start | bytes 1572872 | tf_op jit(solution)/shard_map/ppermute | solution.py:47
  195.4 9.8 %collective-permute-start.27 = (bf16[1,256,256]{2,1,0:T(8,128)(2,1)}, bf16[1,256,256]{2,1,0:T(8,128)(2,1)S(1)}, u32[]{:S(2)}, u32[]{:S(2)}) collective-permute-start(bf16[1,256,256]{2,1,0:T(8,128)(2,1)} %get-tuple-element.85), channel_id=1, source_target_pairs={{0,2},{1,3},{2,4},{3,5},{4,6},{5,7},{6,0},{7,1},{8,10},{9,11},{10,... | collective-permute-start | bytes 393224 | tf_op jit(solution)/shard_map/ppermute | solution.py:47
  195.4 9.9 %collective-permute-start.28 = (bf16[1,256,256]{2,1,0:T(8,128)(2,1)}, bf16[1,256,256]{2,1,0:T(8,128)(2,1)S(1)}, u32[]{:S(2)}, u32[]{:S(2)}) collective-permute-start(bf16[1,256,256]{2,1,0:T(8,128)(2,1)} %get-tuple-element.90), channel_id=1, source_target_pairs={{0,6},{1,7},{2,0},{3,1},{4,2},{5,3},{6,4},{7,5},{8,14},{9,15},{10,... | collective-permute-start | bytes 393224 | tf_op jit(solution)/shard_map/ppermute | solution.py:47
  210.4 9.9 %collective-permute-start.29 = (bf16[1,512,256]{2,1,0:T(8,128)(2,1)}, bf16[1,512,256]{2,1,0:T(8,128)(2,1)S(1)}, u32[]{:S(2)}, u32[]{:S(2)}) collective-permute-start(bf16[1,512,256]{2,1,0:T(8,128)(2,1)} %get-tuple-element.92), channel_id=1, source_target_pairs={{0,2},{1,3},{2,4},{3,5},{4,6},{5,7},{6,0},{7,1},{8,10},{9,11},{10,... | collective-permute-start | bytes 786440 | tf_op jit(solution)/shard_map/ppermute | solution.py:47
  210.5 9.8 %collective-permute-start.30 = (bf16[1,512,256]{2,1,0:T(8,128)(2,1)}, bf16[1,512,256]{2,1,0:T(8,128)(2,1)S(1)}, u32[]{:S(2)}, u32[]{:S(2)}) collective-permute-start(bf16[1,512,256]{2,1,0:T(8,128)(2,1)} %get-tuple-element.96), channel_id=1, source_target_pairs={{0,6},{1,7},{2,0},{3,1},{4,2},{5,3},{6,4},{7,5},{8,14},{9,15},{10,... | collective-permute-start | bytes 786440 | tf_op jit(solution)/shard_map/ppermute | solution.py:47
  (36 other events, 172.1 us)
Sparse Core Ops, SparseCore 0:
  17.7 40.7 all-gather.1
  133.3 73.2 reduce-scatter.1
